TPU v7x, 512 devices: a whole 4x4x16 slice. The times are simulated.
512 devices in a mesh: grp: 8 (over y, core), dev: 64 (over z, x).
Axes of the slice: x: 4, y: 4, z: 16, core: 2. Of those that a mesh axis runs over, the one named last changes fastest.
Arguments:
- right_side: float32 [512, 8192], P('grp', 'dev'), may hold values from -6 to 6
- previous: float32 [512, 8192], P('grp', 'dev'), may hold values from -4 to 4
- east_face: float32 [512, 8192], P('grp', 'dev'), may hold values from 0.5 to 10
- south_face: float32 [512, 8192], P('grp', 'dev'), may hold values from 0.5 to 10
- wet_mask: int32 [512, 8192], P('grp', 'dev'), may hold values from 0 to 1, as said below
Outputs:
- surface: float32 [512, 8192], P('grp', 'dev')
- residual: float32 [512, 8192], P('grp', 'dev')
Inputs may be any that keep to these rules, and one draw needn't show every extreme that they name: `wet_mask`: dry cells form axis-aligned rectangles of 1 to 7 by 1 to 7 cells; each lies inside one aligned tile of 16 x 16 cells, one cell or more away from the tile's border, at most one rectangle a tile.
All inputs are finite; a program needn't handle non-finite values.
Results may differ from a plain program's by a relative error of at most 0.0003.
Values sent between devices are 32-bit elements; how exact they have to be, the bound alone decides.
No kernel may reach another device: no remote copies, remote signals or barrier semaphores. Data moves between devices by JAX's collectives and lax.ppermute only.
A program may use at most 64 MiB of HBM per device.

v0:
```python
import jax
import jax.numpy as jnp
from jax import lax
from jax.sharding import PartitionSpec as P

CYCLES = 2
PRE = 2
POST = 2
COARSE_SWEEPS = 4


relax_weight = 0.8
wet_mass = 2e-05


def extended_2(value, sides, width):
    for axis, dim in sides:
        peers, length = (lax.axis_size(axis), value.shape[dim])
        up = [(i, (i + 1) % peers) for i in range(peers - 1)]
        down = [(j, i) for i, j in up]
        last = lax.slice_in_dim(value, length - width, length, axis=dim)
        initial = lax.slice_in_dim(value, 0, width, axis=dim)
        before = lax.ppermute(last, axis, up)
        after = lax.ppermute(initial, axis, down)
        value = jnp.concatenate([before, value, after], axis=dim)
    return value


def coarsen_sum(values):
    row_count, col_count = values.shape
    return values.reshape(row_count // 2, 2, col_count // 2, 2).sum(axis=(1, 3))


def coarsen_links(coefficients):
    mass_term, east_link, west_link, south_link, north_link = coefficients
    return (
        coarsen_sum(mass_term),
        east_link[0::2, 1::2] + east_link[1::2, 1::2],
        west_link[0::2, 0::2] + west_link[1::2, 0::2],
        south_link[1::2, 0::2] + south_link[1::2, 1::2],
        north_link[0::2, 0::2] + north_link[0::2, 1::2],
    )


def inverse_diagonal(coefficients):
    mass_term, east_link, west_link, south_link, north_link = coefficients
    return 1.0 / (mass_term + east_link + west_link + south_link + north_link)


def operate(padded, coefficients):
    mass_term, east_link, west_link, south_link, north_link = coefficients
    centre = padded[1:-1, 1:-1]
    return (
        mass_term * centre
        + east_link * (centre - padded[1:-1, 2:])
        + west_link * (centre - padded[1:-1, :-2])
        + south_link * (centre - padded[2:, 1:-1])
        + north_link * (centre - padded[:-2, 1:-1])
    )


def jacobi_sweep(values, padded, source, coefficients, inverse):
    return values + relax_weight * (source - operate(padded, coefficients)) * inverse


def zero_padded(values):
    return jnp.pad(values, 1)


def block_padded(values):
    return extended_2(values, (("grp", 0), ("dev", 1)), 1)


def strip_padded(values):
    row_padded = extended_2(values, (("grp", 0),), 1)
    return jnp.pad(row_padded, ((0, 0), (1, 1)))


def prolong(values):
    return jnp.repeat(jnp.repeat(values, 2, axis=0), 2, axis=1)


def smoothing(values, source, coefficients, inverse, sweeps, from_zero, padder):
    for sweep_index in range(sweeps):
        if from_zero and sweep_index == 0:
            values = relax_weight * source * inverse
        else:
            values = jacobi_sweep(values, padder(values), source, coefficients, inverse)
    return values


def unstack(stacked):
    return tuple((stacked[position] for position in range(5)))


def shards(right_side, previous, east_face, south_face, wet_mask):
    group_index = lax.axis_index("grp")
    member_index = lax.axis_index("dev")
    wet = wet_mask.astype(jnp.float32)
    extended = extended_2(jnp.stack([wet, east_face, south_face]), (("grp", 1), ("dev", 2)), 1)
    wet_pad = extended[0]
    east_pad = extended[1]
    south_pad = extended[2]
    east_link = east_face * wet * wet_pad[1:-1, 2:]
    west_link = east_pad[1:-1, :-2] * wet_pad[1:-1, :-2] * wet
    south_link = south_face * wet * wet_pad[2:, 1:-1]
    north_link = south_pad[:-2, 1:-1] * wet_pad[:-2, 1:-1] * wet
    mass_term = wet * wet_mass + (1.0 - wet)
    source = wet * right_side + (1.0 - wet) * previous
    hierarchy = [(mass_term, east_link, west_link, south_link, north_link)]
    for level_index in range(3):
        hierarchy.append(coarsen_links(hierarchy[-1]))
    inverses = [inverse_diagonal(coefficients) for coefficients in hierarchy]
    strip_coefficients = unstack(lax.all_gather(jnp.stack(hierarchy[3]), "dev", axis=2, tiled=True))
    strip_inverse = inverse_diagonal(strip_coefficients)
    coarse_coefficients = coarsen_links(strip_coefficients)
    whole_coefficients = unstack(
        lax.all_gather(jnp.stack(coarse_coefficients), "grp", axis=1, tiled=True)
    )
    whole_inverse = inverse_diagonal(whole_coefficients)
    whole_mass = jnp.sum(whole_coefficients[0])

    def coarse_level(local_source):
        strip_source = lax.all_gather(local_source, "dev", axis=1, tiled=True)
        strip_values = smoothing(
            None, strip_source, strip_coefficients, strip_inverse, PRE, True, strip_padded
        )
        strip_rest = coarsen_sum(
            strip_source - operate(strip_padded(strip_values), strip_coefficients)
        )
        strip_rows = strip_rest.shape[0]
        whole_source = lax.all_gather(strip_rest, "grp", axis=0, tiled=True)
        whole_values = smoothing(
            None, whole_source, whole_coefficients, whole_inverse, COARSE_SWEEPS, True, zero_padded
        )
        whole_rest = whole_source - operate(zero_padded(whole_values), whole_coefficients)
        shift_value = relax_weight * jnp.sum(whole_rest) / whole_mass
        coarse_values = lax.dynamic_slice_in_dim(
            whole_values, group_index * strip_rows, strip_rows, 0
        )
        coarse_values = coarse_values + shift_value
        strip_values = strip_values + prolong(coarse_values)
        strip_values = smoothing(
            strip_values, strip_source, strip_coefficients, strip_inverse, POST, False, strip_padded
        )
        local_width = local_source.shape[1]
        return lax.dynamic_slice_in_dim(strip_values, member_index * local_width, local_width, 1)

    def descend(level_index, values, level_source, from_zero):
        if level_index == 3:
            return coarse_level(level_source)
        coefficients = hierarchy[level_index]
        values = smoothing(
            values, level_source, coefficients, inverses[level_index], PRE, from_zero, block_padded
        )
        remainder = coarsen_sum(level_source - operate(block_padded(values), coefficients))
        values = values + prolong(descend(level_index + 1, None, remainder, True))
        return smoothing(
            values, level_source, coefficients, inverses[level_index], POST, False, block_padded
        )

    surface = previous
    for cycle_index in range(CYCLES):
        surface = descend(0, surface, source, False)
    residual = source - operate(block_padded(surface), hierarchy[0])
    return (surface, residual)


def solution(mesh):
    placed = (P("grp", "dev"), P("grp", "dev"), P("grp", "dev"), P("grp", "dev"), P("grp", "dev"))
    return jax.shard_map(
        shards,
        mesh=mesh,
        in_specs=placed,
        out_specs=(P("grp", "dev"), P("grp", "dev")),
        check_vma=False,
    )
```

profile of v0, /device:TPU:129, one launch (start us, length us, event | category | flops | bytes accessed | tf_op | source)
XLA Modules:
  0.0 903.8 jit_solution(13340431999990689571)
XLA Ops:
  1.4 3.8 collective-permute-start.4
  8.5 3.6 collective-permute-start
  21.1 5.5 collective-permute-start.3
  28.6 3.4 collective-permute-start.7
  33.0 3.6 collective-permute-done.7
  37.7 3.9 collective-permute-start.8
  48.5 3.4 collective-permute-start.11
  53.0 3.6 collective-permute-done.11
  68.0 3.4 collective-permute-start.15
  72.3 3.7 collective-permute-done.15
  78.6 4.8 collective-permute-start.16
  90.3 3.4 collective-permute-start.19
  93.8 4.3 collective-permute-done.19
  108.2 3.4 collective-permute-start.23
  111.8 4.3 collective-permute-done.23
  117.8 82.0 %all_gather.19 = f32[5,8,1024]{1,0,2:T(8,128)S(1)} all-gather(f32[5,8,16]{1,0,2:T(8,128)S(1)} %copy.45), channel_id=1, replica_groups=mesh['grp'=8,'dev'=64] {'dev'}, dimensions={2}, use_global_device_ids=true | all-gather | bytes 166400 | tf_op jit(solution)/shard_map/all_gather | solution.py:114
  208.4 25.2 %collective-permute-start.24 = (f32[1,32]{1,0:T(1,128)S(1)}, f32[1,32]{1,0:T(1,128)S(1)}, u32[]{:S(2)}, u32[]{:S(2)}) collective-permute-start(f32[1,32]{1,0:T(1,128)S(1)} %get-tuple-element.169), channel_id=1, source_target_pairs={{0,64},{64,128},{128,192},{192,256},{256,320},{320,384},{384,448},... | collective-permute-start | bytes 392 | tf_op jit(solution)/shard_map/ppermute | solution.py:23
  238.6 4.3 collective-permute-start.26
  244.8 5.8 collective-permute-done.27
  250.7 3.4 collective-permute-start.28
  261.0 3.4 collective-permute-start.31
  264.4 4.4 collective-permute-done.31
  269.1 59.9 %all-gather = f32[64,16,8]{1,2,0:T(8,128)S(1)} all-gather(f32[1,16,8]{1,2,0:T(8,128)S(1)} %bitcast.353), channel_id=1, replica_groups=mesh['grp'=8,'dev'=64] {'dev'}, dimensions={0}, use_global_device_ids=true | all-gather | bytes 33280 | tf_op jit(solution)/shard_map/all_gather | solution.py:124
  329.3 21.8 %collective-permute-start.32 = (f32[1,1024]{1,0:T(1,128)S(1)}, f32[1,1024]{1,0:T(1,128)S(1)}, u32[]{:S(2)}, u32[]{:S(2)}) collective-permute-start(f32[1,1024]{1,0:T(1,128)S(1)} %get-tuple-element.97), channel_id=1, source_target_pairs={{0,64},{64,128},{128,192},{192,256},{256,320},{320,384},{384,448},... | collective-permute-start | bytes 12296 | tf_op jit(solution)/shard_map/ppermute | solution.py:23
  353.0 14.5 %all_gather.21 = f32[5,32,512]{2,0,1:T(8,128)S(1)} all-gather(f32[5,4,512]{2,0,1:T(8,128)S(1)} %copy.51), channel_id=1, replica_groups=mesh['grp'=8,'dev'=64] {'grp'}, dimensions={1}, use_global_device_ids=true | all-gather | bytes 368640 | tf_op jit(solution)/shard_map/all_gather | solution.py:118
  377.6 11.2 %all-gather.1 = f32[8,4,512]{2,1,0:T(4,128)S(1)} all-gather(f32[1,4,512]{2,1,0:T(4,128)S(1)} %bitcast.350), channel_id=1, replica_groups=mesh['grp'=8,'dev'=64] {'grp'}, dimensions={0}, use_global_device_ids=true | all-gather | bytes 73728 | tf_op jit(solution)/shard_map/all_gather | solution.py:132
  391.8 3.5 collective-permute-start.36
  414.8 4.3 collective-permute-start.42
  421.1 5.8 collective-permute-done.43
  427.0 3.4 collective-permute-start.44
  437.3 3.4 collective-permute-start.47
  440.6 4.4 collective-permute-done.47
  455.4 3.4 collective-permute-start.51
  458.8 4.5 collective-permute-done.51
  473.6 3.4 collective-permute-start.55
  476.9 4.5 collective-permute-done.55
  491.8 3.4 collective-permute-start.59
  495.1 4.6 collective-permute-done.59
  510.1 3.4 collective-permute-start.63
  513.5 4.6 collective-permute-done.63
  528.3 3.4 collective-permute-start.67
  531.6 4.6 collective-permute-done.67
  546.4 3.4 collective-permute-start.71
  549.8 4.6 collective-permute-done.71
  568.0 4.6 collective-permute-done.75
  585.2 3.4 collective-permute-start.79
  588.6 4.5 collective-permute-done.79
  606.6 4.5 collective-permute-done.83
  621.8 3.4 collective-permute-start.87
  625.2 4.4 collective-permute-done.87
  643.1 4.4 collective-permute-done.91
  647.8 60.0 %all-gather.2 = f32[64,16,8]{1,2,0:T(8,128)S(1)} all-gather(f32[1,16,8]{1,2,0:T(8,128)S(1)} %bitcast.354), channel_id=1, replica_groups=mesh['grp'=8,'dev'=64] {'dev'}, dimensions={0}, use_global_device_ids=true | all-gather | bytes 33280 | tf_op jit(solution)/shard_map/all_gather | solution.py:124
  708.0 21.8 %collective-permute-start.92 = (f32[1,1024]{1,0:T(1,128)S(1)}, f32[1,1024]{1,0:T(1,128)S(1)}, u32[]{:S(2)}, u32[]{:S(2)}) collective-permute-start(f32[1,1024]{1,0:T(1,128)S(1)} %get-tuple-element.76), channel_id=1, source_target_pairs={{0,64},{64,128},{128,192},{192,256},{256,320},{320,384},{384,448},... | collective-permute-start | bytes 12296 | tf_op jit(solution)/shard_map/ppermute | solution.py:23
  744.5 11.2 %all-gather.3 = f32[8,4,512]{2,1,0:T(4,128)S(1)} all-gather(f32[1,4,512]{2,1,0:T(4,128)S(1)} %bitcast.349), channel_id=1, replica_groups=mesh['grp'=8,'dev'=64] {'grp'}, dimensions={0}, use_global_device_ids=true | all-gather | bytes 73728 | tf_op jit(solution)/shard_map/all_gather | solution.py:132
  781.3 4.3 collective-permute-start.102
  787.6 5.8 collective-permute-done.103
  793.5 3.4 collective-permute-start.104
  803.8 3.4 collective-permute-start.107
  807.2 4.4 collective-permute-done.107
  825.4 4.5 collective-permute-done.111
  843.5 4.5 collective-permute-done.115
  861.7 4.6 collective-permute-done.119
  880.0 4.6 collective-permute-done.123
  898.2 4.6 collective-permute-done.127
  (503 shorter events, 364.8 us)
Async XLA Ops:
  1.4 12.8 %collective-permute-start.4 = (f32[1,128]{1,0:T(1,128)S(1)}, f32[1,128]{1,0:T(1,128)S(1)}, u32[]{:S(2)}, u32[]{:S(2)}) collective-permute-start(f32[1,128]{1,0:T(1,128)S(1)} %get-tuple-element.105), channel_id=1, source_target_pairs={{0,64},{64,128},{128,192},{192,256},{256,320},{320,384},{384,448},... | collective-permute-start | bytes 1544 | tf_op jit(solution)/shard_map/ppermute | solution.py:23
  5.1 9.0 collective-permute-start.5
  8.5 6.4 collective-permute-start
  18.0 14.0 %collective-permute-start.2 = (f32[3,66,1]{2,1,0:T(8,128)S(1)}, f32[3,66,1]{2,1,0:T(8,128)S(1)}, u32[]{:S(2)}, u32[]{:S(2)}) collective-permute-start(f32[3,66,1]{2,1,0:T(8,128)S(1)} %get-tuple-element.34), channel_id=1, source_target_pairs={{0,1},{1,2},{2,3},{3,4},{4,5},{5,6},{6,7},{7,8},{8,9},{9,10},{10,1... | collective-permute-start | bytes 2384 | tf_op jit(solution)/shard_map/ppermute | solution.py:23
  21.1 10.9 %collective-permute-start.3 = (f32[3,66,1]{2,1,0:T(8,128)S(1)}, f32[3,66,1]{2,1,0:T(8,128)S(1)}, u32[]{:S(2)}, u32[]{:S(2)}) collective-permute-start(f32[3,66,1]{2,1,0:T(8,128)S(1)} %get-tuple-element.35), channel_id=1, source_target_pairs={{1,0},{2,1},{3,2},{4,3},{5,4},{6,5},{7,6},{8,7},{9,8},{10,9},{11,1... | collective-permute-start | bytes 2384 | tf_op jit(solution)/shard_map/ppermute | solution.py:24
  26.7 6.3 collective-permute-start.6
  28.6 8.0 collective-permute-start.7
  37.7 5.9 collective-permute-start.8
  46.6 6.3 collective-permute-start.10
  48.5 8.0 collective-permute-start.11
  56.7 9.3 %collective-permute-start.12 = (f32[1,128]{1,0:T(1,128)S(1)}, f32[1,128]{1,0:T(1,128)S(1)}, u32[]{:S(2)}, u32[]{:S(2)}) collective-permute-start(f32[1,128]{1,0:T(1,128)S(1)} %get-tuple-element.101), channel_id=1, source_target_pairs={{0,64},{64,128},{128,192},{192,256},{256,320},{320,384},{384,448},... | collective-permute-start | bytes 1544 | tf_op jit(solution)/shard_map/ppermute | solution.py:23
  59.8 6.1 collective-permute-start.13
  66.1 6.2 collective-permute-start.14
  68.0 8.0 collective-permute-start.15
  78.6 7.0 collective-permute-start.16
  88.3 5.4 collective-permute-start.18
  90.3 7.8 collective-permute-start.19
  98.2 5.6 collective-permute-start.20
  106.3 5.4 collective-permute-start.22
  108.2 7.8 collective-permute-start.23
  208.4 27.2 %collective-permute-start.24 = (f32[1,32]{1,0:T(1,128)S(1)}, f32[1,32]{1,0:T(1,128)S(1)}, u32[]{:S(2)}, u32[]{:S(2)}) collective-permute-start(f32[1,32]{1,0:T(1,128)S(1)} %get-tuple-element.169), channel_id=1, source_target_pairs={{0,64},{64,128},{128,192},{192,256},{256,320},{320,384},{384,448},... | collective-permute-start | bytes 392 | tf_op jit(solution)/shard_map/ppermute | solution.py:23
  238.6 6.2 collective-permute-start.26
  242.9 7.8 collective-permute-start.27
  250.7 5.4 collective-permute-start.28
  261.0 7.8 collective-permute-start.31
  329.3 38.3 %collective-permute-start.32 = (f32[1,1024]{1,0:T(1,128)S(1)}, f32[1,1024]{1,0:T(1,128)S(1)}, u32[]{:S(2)}, u32[]{:S(2)}) collective-permute-start(f32[1,1024]{1,0:T(1,128)S(1)} %get-tuple-element.97), channel_id=1, source_target_pairs={{0,64},{64,128},{128,192},{192,256},{256,320},{320,384},{384,448},... | collective-permute-start | bytes 12296 | tf_op jit(solution)/shard_map/ppermute | solution.py:23
  351.1 16.4 %collective-permute-start.33 = (f32[1,1024]{1,0:T(1,128)S(1)}, f32[1,1024]{1,0:T(1,128)S(1)}, u32[]{:S(2)}, u32[]{:S(2)}) collective-permute-start(f32[1,1024]{1,0:T(1,128)S(1)} %get-tuple-element.96), channel_id=1, source_target_pairs={{64,0},{128,64},{192,128},{256,192},{320,256},{384,320},{448,384},... | collective-permute-start | bytes 12296 | tf_op jit(solution)/shard_map/ppermute | solution.py:24
  391.8 5.6 collective-permute-start.36
  414.8 6.3 collective-permute-start.42
  419.1 7.8 collective-permute-start.43
  427.0 5.4 collective-permute-start.44
  437.3 7.8 collective-permute-start.47
  453.5 5.3 collective-permute-start.50
  455.4 7.8 collective-permute-start.51
  471.6 5.3 collective-permute-start.54
  473.6 7.8 collective-permute-start.55
  489.8 5.3 collective-permute-start.58
  491.8 8.0 collective-permute-start.59
  508.2 5.3 collective-permute-start.62
  510.1 8.0 collective-permute-start.63
  526.3 5.3 collective-permute-start.66
  528.3 8.0 collective-permute-start.67
  544.5 5.3 collective-permute-start.70
  546.4 8.0 collective-permute-start.71
  562.7 5.3 collective-permute-start.74
  564.6 8.0 collective-permute-start.75
  583.3 5.3 collective-permute-start.78
  585.2 7.8 collective-permute-start.79
  603.2 7.8 collective-permute-start.83
  621.8 7.8 collective-permute-start.87
  639.7 7.8 collective-permute-start.91
  708.0 23.7 %collective-permute-start.92 = (f32[1,1024]{1,0:T(1,128)S(1)}, f32[1,1024]{1,0:T(1,128)S(1)}, u32[]{:S(2)}, u32[]{:S(2)}) collective-permute-start(f32[1,1024]{1,0:T(1,128)S(1)} %get-tuple-element.76), channel_id=1, source_target_pairs={{0,64},{64,128},{128,192},{192,256},{256,320},{320,384},{384,448},... | collective-permute-start | bytes 12296 | tf_op jit(solution)/shard_map/ppermute | solution.py:23
  781.3 6.3 collective-permute-start.102
  785.7 7.8 collective-permute-start.103
  793.5 5.4 collective-permute-start.104
  803.8 7.8 collective-permute-start.107
  822.0 7.8 collective-permute-start.111
  840.1 7.8 collective-permute-start.115
  856.4 5.3 collective-permute-start.118
  858.3 8.0 collective-permute-start.119
  874.7 5.3 collective-permute-start.122
  876.7 8.0 collective-permute-start.123
  892.9 5.3 collective-permute-start.126
  894.8 8.0 collective-permute-start.127
  (76 other events, 1024.0 us)
where the time goes:
time: 915 us; the launch traced here: 904 us
  starting transfers between devices  397 us (43%)
  blocking collectives  239 us (26%)
  waiting for transfers between devices  215 us (23%)
  local copies, waits for them, and re-layouts  30.7 us (3%)
  other arithmetic  16.4 us (2%)
    ppermute x64, starting transfers between devices, extended_2(): before = lax.ppermute(last, axis, up)  261 us
    ppermute x64, starting transfers between devices, extended_2(): after = lax.ppermute(initial, axis, down)  136 us
    ppermute x64, waiting for transfers between devices, extended_2(): before = lax.ppermute(last, axis, up)  123 us
    all_gather x2, blocking collectives, coarse_level(): strip_source = lax.all_gather(local_source, 'dev', axis=1, tiled=True)  120 us
    ppermute x64, waiting for transfers between devices, extended_2(): after = lax.ppermute(initial, axis, down)  91.6 us
    all_gather x1, blocking collectives, shards(): lax.all_gather(jnp.stack(hierarchy[3]), 'dev', axis=2, tiled=True)  82 us
    all_gather x2, blocking collectives, coarse_level(): whole_source = lax.all_gather(strip_rest, 'grp', axis=0, tiled=True)  22.4 us
  transfers between devices with their start and end apart: 128, of which 60 were waited for; matrix products, arithmetic and copies ran while one was open for 1% of the time, Pallas kernels for 0%

commit v1 on v0

v1 whole, which is shorter than its diff:
```python
import jax
import jax.numpy as jnp
from jax import lax
from jax.experimental import pallas as pl
from jax.experimental.pallas import tpu as pltpu
from jax.sharding import Mesh
from jax.sharding import PartitionSpec as P

F32 = jnp.float32
RELAX = 0.8
WET_MASS = 2e-05
PAD = 8
CHUNK = 32
EAST, WEST, SOUTH, NORTH, MASS, RATE = range(6)


def lanes(shape):
    return lax.broadcasted_iota(jnp.int32, shape, len(shape) - 1)


def from_east(x, step):
    return pltpu.roll(x, x.shape[1] - step, 1)


def from_west(x, step):
    return pltpu.roll(x, step, 1)


def first_of_pair(x, step):
    return (lanes(x.shape) & step) == 0


def pair_sum(x, step):
    return x + jnp.where(first_of_pair(x, step), from_east(x, step), from_west(x, step))


def get(ref, start, count, *at):
    return jnp.concatenate([ref[(*at, h, pl.ds(start, count), slice(None))] for h in range(ref.shape[len(at)])], axis=1)


def get_strided(ref, start, count, *at):
    return jnp.concatenate(
        [ref[(*at, h, pl.ds(start, count, stride=2), slice(None))] for h in range(ref.shape[len(at)])], axis=1
    )


def put(ref, start, value, *at):
    for h in range(ref.shape[len(at)]):
        ref[(*at, h, pl.ds(start, value.shape[0]), slice(None))] = value[:, 128 * h : 128 * h + 128]


def chunks(low, high, size=CHUNK):
    return [(a, min(size, high - a)) for a in range(low, high, size)]


def clear(*refs):
    for ref in refs:
        ref[...] = jnp.zeros(ref.shape, F32)


def operate(v_ref, co, a, n, step):
    v = get(v_ref, PAD + a, n)
    out = (
        get(co, a, n, MASS) * v
        + get(co, a, n, EAST) * (v - from_east(v, step))
        + get(co, a, n, WEST) * (v - from_west(v, step))
        + get(co, a, n, SOUTH) * (v - get(v_ref, PAD + a + 1, n))
        + get(co, a, n, NORTH) * (v - get(v_ref, PAD + a - 1, n))
    )
    return v, out


def sweep(v_ref, to, co, b_ref, low, high, step):
    for a, n in chunks(low, high):
        v, out = operate(v_ref, co, a, n, step)
        rest = -out if b_ref is None else get(b_ref, a, n) - out
        put(to, PAD + a, v + rest * get(co, a, n, RATE))


def first_sweep(to, co, b_ref, low, high):
    for a, n in chunks(low, high):
        put(to, PAD + a, get(b_ref, a, n) * get(co, a, n, RATE))


def residual(v_ref, to, co, b_ref, low, high, step):
    for a, n in chunks(low, high):
        _, out = operate(v_ref, co, a, n, step)
        put(to, a, -out if b_ref is None else get(b_ref, a, n) - out)


def block_sum(fine, a, n, step, *at):
    return pair_sum(get_strided(fine, 2 * a, n, *at) + get_strided(fine, 2 * a + 1, n, *at), step)


def restrict(fine, to, low, high, step):
    for a, n in chunks(low // 2, high // 2):
        put(to, a, block_sum(fine, a, n, step))


def prolong(coarse, base, to, low, high):
    for a, n in chunks(low // 2, high // 2):
        value = get(coarse, PAD + a, n)
        for p in range(2):
            for h in range(to.shape[0]):
                part = value[:, 128 * h : 128 * h + 128]
                rows = pl.ds(PAD + 2 * a + p, n, stride=2)
                to[h, rows, :] = part if base is None else base[h, rows, :] + part


def diagonal(co, a, n):
    total = get(co, a, n, MASS)
    for k in (EAST, WEST, SOUTH, NORTH):
        total = total + get(co, a, n, k)
    return total


def coarsen(fine, to, rows, step):
    for a, n in chunks(0, rows):
        put(to, a, block_sum(fine, a, n, step, MASS), MASS)
        east = get_strided(fine, 2 * a, n, EAST) + get_strided(fine, 2 * a + 1, n, EAST)
        put(to, a, jnp.where(first_of_pair(east, step), from_east(east, step), east), EAST)
        west = get_strided(fine, 2 * a, n, WEST) + get_strided(fine, 2 * a + 1, n, WEST)
        put(to, a, jnp.where(first_of_pair(west, step), west, from_west(west, step)), WEST)
        put(to, a, pair_sum(get_strided(fine, 2 * a + 1, n, SOUTH), step), SOUTH)
        put(to, a, pair_sum(get_strided(fine, 2 * a, n, NORTH), step), NORTH)


def set_rate(co, rows):
    for a, n in chunks(0, rows):
        d = diagonal(co, a, n)
        put(co, a, RELAX / jnp.where(d > 0, d, 1.0), RATE)


def field(*shape):
    return jax.ShapeDtypeStruct(shape, F32)


def scratch(*shape):
    return pltpu.VMEM(shape, F32)


def call(body, outs, scratches, *args):
    vmem = pl.BlockSpec(memory_space=pltpu.VMEM)
    return pl.pallas_call(
        body,
        out_shape=outs,
        in_specs=[vmem] * len(args),
        out_specs=jax.tree.map(lambda _: vmem, outs),
        scratch_shapes=scratches,
        compiler_params=pltpu.CompilerParams(vmem_limit_bytes=28 * 1024 * 1024),
    )(*args)


def prepare(right, previous, east, south, mask, own, to_east, to_west):
    wet = mask[...] > 0
    own[0] = jnp.where(wet, east[...], 0.0)
    own[1] = jnp.where(wet, south[...], 0.0)
    own[2] = jnp.where(wet, right[...], previous[...])
    own[3] = previous[...]
    low = lanes((64, 128)) < 64
    for k in range(2):
        a, b = own[2 * k], pltpu.roll(own[2 * k + 1], 64, 1)
        to_east[k] = jnp.where(low, b, a)
        to_west[k] = jnp.where(low, a, b)


def widen(own, west, east, out):
    low = lanes((64, 128)) < 64
    for k in range(2):
        e, w = east[k], west[k]
        out[2 * k] = own[2 * k]
        out[2 * k + 1] = own[2 * k + 1]
        out[4 + 2 * k] = jnp.where(low, e, w)
        out[5 + 2 * k] = jnp.where(low, pltpu.roll(e, 64, 1), pltpu.roll(w, 64, 1))


def descend(v1_ref, v2_ref, b1_ref, b2_ref, b3_ref, co, rest, temp, ranges):
    (l0, h0), (l1, h1), (l2, h2), (l3, h3) = ranges
    restrict(rest[0], b1_ref, l0, h0, 1)
    first_sweep(temp[1], co[1], b1_ref, l1, h1)
    sweep(temp[1], v1_ref, co[1], b1_ref, l1, h1, 2)
    residual(v1_ref, rest[1], co[1], b1_ref, l1, h1, 2)
    restrict(rest[1], b2_ref, l1, h1, 2)
    first_sweep(temp[2], co[2], b2_ref, l2, h2)
    sweep(temp[2], v2_ref, co[2], b2_ref, l2, h2, 4)
    residual(v2_ref, rest[2], co[2], b2_ref, l2, h2, 4)
    restrict(rest[2], b3_ref, l3, h3, 4)


def first_leg(own, up, down, co0, co1, co2, b0, b1, b2, v0, v1, v2, packed, *temps):
    wet_ref, south_ref, t0, t1, t2, r0, r1, r2, b3, co3 = temps
    clear(wet_ref, south_ref, t0, t1, t2, v0, v1, v2)
    parts = (up, own, down)

    def window(k, a, n):
        ref, o = parts[a // 64], a % 64
        return jnp.concatenate([ref[k, o : o + n, :], ref[4 + k, o : o + n, :]], axis=1)

    for a, n in chunks(0, 192):
        put(wet_ref, PAD + a, jnp.where(window(0, a, n) > 0, 1.0, 0.0))
        put(v0, PAD + a, window(3, a, n))
        put(b0, a, window(2, a, n))
    for a, n in chunks(0, 192):
        wet = get(wet_ref, PAD + a, n)
        east = window(0, a, n) * from_east(wet, 1)
        south = window(1, a, n) * get(wet_ref, PAD + a + 1, n)
        put(co0, a, east, EAST)
        put(co0, a, from_west(east, 1), WEST)
        put(co0, a, south, SOUTH)
        put(south_ref, PAD + a, south)
        put(co0, a, wet * WET_MASS + (1.0 - wet), MASS)
    for a, n in chunks(0, 192):
        put(co0, a, get(south_ref, PAD + a - 1, n), NORTH)
    set_rate(co0, 192)
    coarsen(co0, co1, 96, 1)
    set_rate(co1, 96)
    coarsen(co1, co2, 48, 2)
    set_rate(co2, 48)
    coarsen(co2, co3, 24, 4)
    sweep(v0, t0, co0, b0, 0, 192, 1)
    sweep(t0, v0, co0, b0, 0, 192, 1)
    residual(v0, r0, co0, b0, 0, 192, 1)
    descend(
        v1, v2, b1, b2, b3, (co0, co1, co2), (r0, r1, r2), (t0, t1, t2), ((0, 192), (0, 96), (0, 48), (16, 32))
    )
    slot = lanes((8, 128)) & 7
    values = (
        b3[0, 8:16, :],
        co3[MASS, 0, 8:16, :],
        co3[EAST, 0, 8:16, :],
        co3[SOUTH, 0, 8:16, :],
        diagonal(co3, 8, 8)[:, :128],
    )
    out = jnp.zeros((8, 128), F32)
    for k, value in enumerate(values):
        out = jnp.where(slot == k, value, out)
    packed[...] = out


def fan_row(west, own, east, out):
    for g in range(out.shape[0]):
        out[g, 0] = west[...]
        out[g, 1] = own[...]
        out[g, 2] = east[...]


def spread(x, slot):
    y = jnp.where((lanes(x.shape) & 7) == slot, x, 0.0)
    for step in (1, 2, 4):
        y = pair_sum(y, step)
    return y


def inner_part(wide, to):
    to[0, pl.ds(PAD, 24), :] = wide[1, pl.ds(PAD + 8, 24), :]
    low = lanes((24, 128)) < 64
    to[1, pl.ds(PAD, 24), :] = jnp.where(low, wide[2, pl.ds(PAD + 8, 24), :], wide[0, pl.ds(PAD + 8, 24), :])


def solve_coarse(b3, b4, co3, co4, v3, s3, v4, s4, rest, shift):
    first_sweep(s3, co3, b3, 0, 40)
    sweep(s3, v3, co3, b3, 0, 40, 8)
    residual(v3, rest, co3, b3, 0, 40, 8)
    restrict(rest, b4, 0, 48, 8)
    first_sweep(s4, co4, b4, 0, 24)
    sweep(s4, v4, co4, b4, 0, 24, 16)
    sweep(v4, s4, co4, b4, 0, 24, 16)
    sweep(s4, v4, co4, b4, 0, 24, 16)
    if shift is not None:
        put(v4, PAD, get(v4, PAD, 24) + shift)
    prolong(v4, v3, v3, 0, 40)
    sweep(v3, s3, co3, b3, 0, 40, 8)
    sweep(s3, v3, co3, b3, 0, 40, 8)


def second_leg(gathered, co0, co1, co2, b0, b1, b2, v0, v1, v2, *others):
    (v0a, v0b, v1a, v1b, v2a, v2b, b1a, b1b, b2a, b2b, co3, co4, packed, *temps) = others
    (t0, s0, u0, t1, s1, u1, t2, s2, u2, r0, r1, r2, e3, u3, bn, b3, b4, v3, s3, w3, v4, s4, r3, south_ref) = temps
    clear(t0, s0, u0, t1, s1, u1, t2, s2, u2, e3, u3, v3, s3, w3, v4, s4, r3, south_ref, co4)
    clear(v0a, v0b, v1a, v1b, v2a, v2b)
    group = lax.axis_index("grp")
    for t in range(5):
        at = group + (t - 2)
        valid = jnp.logical_and(at >= 0, at < 8).astype(F32)
        at = jnp.clip(at, 0, 7)
        x = jnp.concatenate([gathered[at, k] for k in range(3)], axis=1) * valid
        row = 8 * t
        put(b3, row, spread(x, 0))
        put(co3, row, spread(x, 1), MASS)
        east = spread(x, 2)
        put(co3, row, east, EAST)
        put(co3, row, from_west(east, 8), WEST)
        south = spread(x, 3)
        put(co3, row, south, SOUTH)
        put(south_ref, PAD + row, south)
        d = spread(x, 4)
        put(co3, row, RELAX / jnp.where(d > 0, d, 1.0), RATE)
    for a, n in chunks(0, 40):
        put(co3, a, get(south_ref, PAD + a - 1, n), NORTH)
    coarsen(co3, co4, 20, 8)
    set_rate(co4, 24)

    put(v4, PAD, jnp.ones((24, 384), F32))
    for here, there in ((v4, s4), (s4, v4), (v4, s4), (s4, v4)):
        sweep(here, there, co4, None, 0, 24, 16)
    prolong(v4, None, w3, 0, 40)
    sweep(w3, s3, co3, None, 0, 40, 8)
    sweep(s3, w3, co3, None, 0, 40, 8)
    weight = w3[1, pl.ds(PAD + 16, 8), :]

    solve_coarse(b3, b4, co3, co4, v3, s3, v4, s4, r3, None)
    inner_part(v3, e3)
    put(v3, PAD, jnp.ones((40, 384), F32))
    sweep(v3, s3, co3, None, 0, 40, 8)
    sweep(s3, v3, co3, None, 0, 40, 8)
    inner_part(v3, u3)
    for base, coarse, b_ref, level in ((v2, e3, b2, 0), (None, u3, None, 1)):
        e2, e1, e0 = (t2, t1, t0) if level == 0 else (u2, u1, u0)
        prolong(coarse, base, e2, 0, 48)
        sweep(e2, s2, co2, b_ref, 0, 48, 4)
        sweep(s2, e2, co2, b_ref, 0, 48, 4)
        prolong(e2, None if base is None else v1, e1, 8, 88)
        sweep(e1, s1, co1, None if base is None else b1, 8, 88, 2)
        sweep(s1, e1, co1, None if base is None else b1, 8, 88, 2)
        prolong(e1, None if base is None else v0, e0, 32, 160)
        sweep(e0, s0, co0, None if base is None else b0, 32, 160, 1)
        sweep(s0, e0, co0, None if base is None else b0, 32, 160, 1)

    source = b3[1, 16:24, :]
    mass = co3[MASS, 1, 16:24, :]
    results = []
    for start, b_ref, x0, x1, x2, y1, y2 in ((t0, b0, v0a, v1a, v2a, b1a, b2a), (u0, None, v0b, v1b, v2b, b1b, b2b)):
        clear(s0, s1, s2)
        sweep(start, s0, co0, b_ref, 32, 160, 1)
        sweep(s0, x0, co0, b_ref, 32, 160, 1)
        residual(x0, r0, co0, b_ref, 32, 160, 1)
        descend(
            x1, x2, y1, y2, bn, (co0, co1, co2), (r0, r1, r2), (s0, s1, s2), ((32, 160), (16, 80), (8, 40), (16, 32))
        )
        results.append(bn[0, 8:16, :])
    place = lanes((8, 128))
    out = jnp.where((place & 7) == 0, results[0], jnp.where((place & 7) == 1, results[1], 0.0))
    sums = (mass, weight * source, weight * results[0], weight * results[1])
    for k, value in enumerate(sums):
        once = jnp.where((place & 7) == 0, value, 0.0)
        total = jnp.sum(jnp.sum(once, axis=0, keepdims=True), axis=1, keepdims=True)
        out = jnp.where(place == 8 * k + 6, total, out)
    for z in range(packed.shape[0]):
        packed[z] = out


def relay(gathered, out):
    z = lax.axis_index("z")
    last = gathered.shape[0] - 1
    own = gathered[z]
    before = gathered[jnp.maximum(z - 1, 0)]
    after = gathered[jnp.minimum(z + 1, last)]
    total = gathered[0]
    for k in range(1, last + 1):
        total = total + gathered[k]
    slot = lanes((8, 128)) & 7
    value = jnp.where(slot < 2, own, jnp.where(slot < 4, pltpu.roll(before, 2, 1), pltpu.roll(after, 4, 1)))
    value = jnp.where(slot < 6, value, total)
    for k in range(out.shape[0]):
        out[k] = value


def third_leg(gathered, co0, co1, co2, b0, v0a, v0b, v1a, v1b, v2a, v2b, b1a, b1b, b2a, b2b, co3, co4, *others):
    (surface, rest, *temps) = others
    (t0, s0, c0, t1, s1, c1, d1, t2, s2, c2, d2, e3, b3, b4, v3, s3, v4, s4, r3) = temps
    clear(t0, s0, c0, t1, s1, c1, t2, s2, c2, e3, v3, s3, v4, s4, r3)
    total = gathered[0]
    for k in range(1, gathered.shape[0]):
        total = total + gathered[k]
    place = lanes((1, 128))
    mass, sum1, sum2a, sum2b = (
        jnp.sum(jnp.where(place == 8 * k + 6, total[:1], 0.0), axis=1, keepdims=True) for k in range(4)
    )
    shift1 = RELAX * sum1 / mass
    shift2 = RELAX * (sum2a + shift1 * sum2b) / mass

    group, x = lax.axis_index("grp"), lax.axis_index("x")
    inner_west, inner_east = x > 0, x < 3
    at_west = jnp.where(inner_west, x - 1, 3)
    at_east = jnp.where(inner_east, x + 1, 0)
    for t in range(5):
        g = 4 * jnp.clip(group + (t - 2), 0, 7)
        w, o, e = gathered[g + at_west], gathered[g + x], gathered[g + at_east]
        w = jnp.where(inner_west, w, pltpu.roll(w, 126, 1))
        e = jnp.where(inner_east, e, pltpu.roll(e, 124, 1))
        both = jnp.concatenate([w, o, e], axis=1)
        put(b3, 8 * t, spread(both + shift1 * from_east(both, 1), 0))
    solve_coarse(b3, b4, co3, co4, v3, s3, v4, s4, r3, shift2)
    inner_part(v3, e3)

    def combine(to, first, second, offset, low, high):
        for a, n in chunks(offset + low, offset + high):
            put(to, a, get(first, a, n) + shift1 * get(second, a, n))

    combine(c2, v2a, v2b, PAD, 8, 40)
    combine(d2, b2a, b2b, 0, 8, 40)
    combine(c1, v1a, v1b, PAD, 24, 72)
    combine(d1, b1a, b1b, 0, 24, 72)
    combine(c0, v0a, v0b, PAD, 56, 136)
    prolong(e3, c2, t2, 8, 40)
    sweep(t2, s2, co2, d2, 8, 40, 4)
    sweep(s2, t2, co2, d2, 8, 40, 4)
    prolong(t2, c1, t1, 24, 72)
    sweep(t1, s1, co1, d1, 24, 72, 2)
    sweep(s1, t1, co1, d1, 24, 72, 2)
    prolong(t1, c0, t0, 56, 136)
    sweep(t0, s0, co0, b0, 56, 136, 1)
    sweep(s0, t0, co0, b0, 56, 136, 1)
    surface[...] = t0[0, pl.ds(PAD + 64, 64), :]
    for a, n in chunks(64, 128):
        _, out = operate(t0, co0, a, n, 1)
        rest[a - 64 : a - 64 + n, :] = b0[0, a : a + n, :] - out[:, :128]


def shards(right_side, previous, east_face, south_face, wet_mask):
    dev = ("z", "x")
    to_next = [(i, i + 1) for i in range(63)]
    to_last = [(j, i) for i, j in to_next]
    own, to_east, to_west = call(
        prepare,
        (field(4, 64, 128), field(2, 64, 128), field(2, 64, 128)),
        [],
        right_side,
        previous,
        east_face,
        south_face,
        wet_mask,
    )
    west = lax.ppermute(to_east, dev, to_next)
    east = lax.ppermute(to_west, dev, to_last)
    own = call(widen, field(8, 64, 128), [], own, west, east)
    up = lax.ppermute(own, "grp", to_next[:7])
    down = lax.ppermute(own, "grp", to_last[:7])

    def rows(count, planes=2):
        return field(planes, count, 128)

    def shifted(count, planes=2):
        return field(planes, count + 2 * PAD, 128)

    def as_scratch(*fields):
        return [scratch(*f.shape) for f in fields]

    co = [field(6, 2, count, 128) for count in (192, 96, 48)]
    *kept, packed = call(
        first_leg,
        (*co, rows(192), rows(96), rows(48), shifted(192), shifted(96), shifted(48), field(8, 128)),
        as_scratch(
            shifted(192),
            shifted(192),
            shifted(192),
            shifted(96),
            shifted(48),
            rows(192),
            rows(96),
            rows(48),
            rows(24),
            field(6, 2, 24, 128),
        ),
        own,
        up,
        down,
    )
    west = lax.ppermute(packed, dev, to_next)
    east = lax.ppermute(packed, dev, to_last)
    gathered = call(fan_row, field(8, 3, 8, 128), [], west, packed, east)
    gathered = lax.all_to_all(gathered, "grp", 0, 0, tiled=True)
    wide = [shifted(40, 3), shifted(40, 3), shifted(40, 3), shifted(24, 3), shifted(24, 3)]
    *second, packed = call(
        second_leg,
        (
            shifted(192),
            shifted(192),
            shifted(96),
            shifted(96),
            shifted(48),
            shifted(48),
            rows(96),
            rows(96),
            rows(48),
            rows(48),
            field(6, 3, 40, 128),
            field(6, 3, 24, 128),
            field(16, 8, 128),
        ),
        as_scratch(
            *[shifted(192)] * 3,
            *[shifted(96)] * 3,
            *[shifted(48)] * 3,
            rows(192),
            rows(96),
            rows(48),
            shifted(24),
            shifted(24),
            rows(24),
            rows(40, 3),
            rows(24, 3),
            *wide,
            rows(48, 3),
            shifted(40, 3),
        ),
        gathered,
        *kept,
    )
    gathered = lax.all_to_all(packed, "z", 0, 0, tiled=True)
    gathered = call(relay, field(32, 8, 128), [], gathered)
    gathered = lax.all_to_all(gathered, ("grp", "x"), 0, 0, tiled=True)
    surface, rest = call(
        third_leg,
        (field(64, 128), field(64, 128)),
        as_scratch(
            *[shifted(192)] * 3,
            *[shifted(96)] * 3,
            rows(96),
            *[shifted(48)] * 3,
            rows(48),
            shifted(24),
            rows(40, 3),
            rows(24, 3),
            shifted(40, 3),
            shifted(40, 3),
            shifted(24, 3),
            shifted(24, 3),
            rows(48, 3),
        ),
        gathered,
        *kept[:4],
        *second,
    )
    return surface, rest


def solution(mesh):
    split = Mesh(mesh.devices.reshape(8, 16, 4), ("grp", "z", "x"))
    placed = P("grp", ("z", "x"))
    return jax.shard_map(shards, mesh=split, in_specs=(placed,) * 5, out_specs=(placed,) * 2, check_vma=False)
```

time: 915 us -> 103 us (0.11)
  the two profiles are of different devices: /device:TPU:129 before, /device:TPU:1 now
where the time goes in v1:
time: 103 us; the launch traced here: 102 us
  blocking collectives  59.3 us (58%)
  starting transfers between devices  19.7 us (19%)
  Pallas kernels  11.1 us (11%)
  waiting for transfers between devices  7.73 us (8%)
  local copies, waits for them, and re-layouts  3.78 us (4%)
    all_to_all x1, blocking collectives, shards(): gathered = lax.all_to_all(packed, 'z', 0, 0, tiled=True)  36.6 us
    all_to_all x1, blocking collectives, shards(): gathered = lax.all_to_all(gathered, ('grp', 'x'), 0, 0, tiled=True)  12.6 us
    pallas_call x7, Pallas kernels, call(): pl.pallas_call(body, out_shape=outs, in_specs=[vmem] * len(args), out_spe...  11.1 us
    all_to_all x1, blocking collectives, shards(): gathered = lax.all_to_all(gathered, 'grp', 0, 0, tiled=True)  10 us
    ppermute x1, starting transfers between devices, shards(): down = lax.ppermute(own, 'grp', to_last[:7])  7.28 us
    ppermute x1, starting transfers between devices, shards(): west = lax.ppermute(packed, dev, to_next)  3.99 us
    ppermute x1, starting transfers between devices, shards(): west = lax.ppermute(to_east, dev, to_next)  3.95 us
    unnamed x10, local copies, waits for them, and re-layouts  3.78 us
  transfers between devices with their start and end apart: 6, of which 3 were waited for; matrix products, arithmetic and copies ran while one was open for 0% of the time, Pallas kernels for 0%

profile of v1, /device:TPU:1, one launch (start us, length us, event | category | flops | bytes accessed | tf_op | source)
XLA Modules:
  0.0 102.3 jit_solution(14394301782292199544)
XLA Ops:
  0.6 0.0 copy-start
  0.6 0.7 copy-done
  1.4 0.0 copy-start.1
  1.4 0.8 copy-done.1
  2.1 0.0 copy-start.2
  2.2 0.8 copy-done.2
  2.9 0.0 copy-start.3
  2.9 0.8 copy-done.3
  3.7 0.0 copy-start.4
  3.7 0.8 copy-done.4
  4.4 0.1 shard_map.68
  4.5 3.9 %collective-permute-start = (f32[2,64,128]{2,1,0:T(8,128)S(1)}, f32[2,64,128]{2,1,0:T(8,128)S(1)}, u32[]{:S(2)}, u32[]{:S(2)}) collective-permute-start(f32[2,64,128]{2,1,0:T(8,128)S(1)} %get-tuple-element.29), channel_id=1, source_target_pairs={{0,1},{1,2},{2,3},{3,4},{4,5},{5,6},{6,7},{7,8},{8,9},{9,10},{10,1... | collective-permute-start | bytes 196616 | tf_op jit(solution)/shard_map/ppermute | solution.py:434
  8.5 1.3 %collective-permute-start.1 = (f32[2,64,128]{2,1,0:T(8,128)S(1)}, f32[2,64,128]{2,1,0:T(8,128)S(1)}, u32[]{:S(2)}, u32[]{:S(2)}) collective-permute-start(f32[2,64,128]{2,1,0:T(8,128)S(1)} %get-tuple-element.30), channel_id=1, source_target_pairs={{1,0},{2,1},{3,2},{4,3},{5,4},{6,5},{7,6},{8,7},{9,8},{10,9},{11,1... | collective-permute-start | bytes 196616 | tf_op jit(solution)/shard_map/ppermute | solution.py:435
  9.8 0.0 collective-permute-done.west
  9.8 3.7 %collective-permute-done.1.east = f32[2,64,128]{2,1,0:T(8,128)S(1)} collective-permute-done((f32[2,64,128]{2,1,0:T(8,128)S(1)}, f32[2,64,128]{2,1,0:T(8,128)S(1)}, u32[]{:S(2)}, u32[]{:S(2)}) %collective-permute-start.1) | collective-permute-done | bytes 65568 | tf_op jit(solution)/shard_map/ppermute | solution.py:435
  13.5 0.1 shard_map.69.own
  13.6 7.3 %collective-permute-start.3 = (f32[8,64,128]{2,1,0:T(8,128)S(1)}, f32[8,64,128]{2,1,0:T(8,128)S(1)}, u32[]{:S(2)}, u32[]{:S(2)}) collective-permute-start(f32[8,64,128]{2,1,0:T(8,128)S(1)} %shard_map.69.own), channel_id=1, source_target_pairs={{64,0},{128,64},{192,128},{256,192},{320,256},{384,320},{448,384},... | collective-permute-start | bytes 786440 | tf_op jit(solution)/shard_map/ppermute | solution.py:438
  20.9 1.9 %collective-permute-start.2 = (f32[8,64,128]{2,1,0:T(8,128)S(1)}, f32[8,64,128]{2,1,0:T(8,128)S(1)}, u32[]{:S(2)}, u32[]{:S(2)}) collective-permute-start(f32[8,64,128]{2,1,0:T(8,128)S(1)} %shard_map.69.own), channel_id=1, source_target_pairs={{0,64},{64,128},{128,192},{192,256},{256,320},{320,384},{384,448},... | collective-permute-start | bytes 786440 | tf_op jit(solution)/shard_map/ppermute | solution.py:437
  22.8 0.0 collective-permute-done.3.down
  22.8 3.3 %collective-permute-done.2.up = f32[8,64,128]{2,1,0:T(8,128)S(1)} collective-permute-done((f32[8,64,128]{2,1,0:T(8,128)S(1)}, f32[8,64,128]{2,1,0:T(8,128)S(1)}, u32[]{:S(2)}, u32[]{:S(2)}) %collective-permute-start.2) | collective-permute-done | bytes 262176 | tf_op jit(solution)/shard_map/ppermute | solution.py:437
  26.1 1.5 %shard_map.70 = (f32[6,2,192,128]{3,2,1,0:T(8,128)S(1)}, f32[6,2,96,128]{3,2,1,0:T(8,128)S(1)}, f32[6,2,48,128]{3,2,1,0:T(8,128)S(1)}, f32[2,192,128]{2,1,0:T(8,...) custom-call(f32[8,64,128]{2,1,0:T(8,128)S(1)} %shard_map.69.own, ...), custom_call_target="tpu_custom_call" | custom-call | tf_op jit(solution)/shard_map/pallas_call | solution.py:144
  27.6 1.3 %collective-permute-start.5 = (f32[8,128]{1,0:T(8,128)S(1)}, f32[8,128]{1,0:T(8,128)S(1)}, u32[]{:S(2)}, u32[]{:S(2)}) collective-permute-start(f32[8,128]{1,0:T(8,128)S(1)} %get-tuple-element.31.own), channel_id=1, source_target_pairs={{1,0},{2,1},{3,2},{4,3},{5,4},{6,5},{7,6},{8,7},{9,8},{10,9},{11,1... | collective-permute-start | bytes 12296 | tf_op jit(solution)/shard_map/ppermute | solution.py:470
  28.9 4.0 %collective-permute-start.4 = (f32[8,128]{1,0:T(8,128)S(1)}, f32[8,128]{1,0:T(8,128)S(1)}, u32[]{:S(2)}, u32[]{:S(2)}) collective-permute-start(f32[8,128]{1,0:T(8,128)S(1)} %get-tuple-element.31.own), channel_id=1, source_target_pairs={{0,1},{1,2},{2,3},{3,4},{4,5},{5,6},{6,7},{7,8},{8,9},{9,10},{10,1... | collective-permute-start | bytes 12296 | tf_op jit(solution)/shard_map/ppermute | solution.py:469
  32.9 0.0 collective-permute-done.5.east
  32.9 0.7 collective-permute-done.4.west
  33.6 10.0 %all_to_all.15.gathered = f32[8,3,8,128]{3,2,1,0:T(8,128)S(1)} all-to-all(f32[8,3,8,128]{3,2,1,0:T(8,128)S(1)} %shard_map.71), channel_id=1, replica_groups=mesh['grp'=8,'z'=16,'x'=4] {'grp'}, dimensions={0} | all-to-all | bytes 196608 | tf_op jit(solution)/shard_map/all_to_all | solution.py:472
  43.7 6.7 %shard_map.72 = (f32[2,208,128]{2,1,0:T(8,128)S(1)}, f32[2,208,128]{2,1,0:T(8,128)S(1)}, f32[2,112,128]{2,1,0:T(8,128)S(1)}, f32[2,112,128]{2,1,0:T(8,128)S(1)},...) custom-call(f32[8,3,8,128]{3,2,1,0:T(8,128)S(1)} %all_to_all.15.gath, ...), custom_call_target="tpu_custom_call" | custom-call | tf_op jit(solution)/shard_map/pallas_call | solution.py:144
  50.4 36.6 %all_to_all.16.gathered = f32[16,8,128]{2,1,0:T(8,128)S(1)} all-to-all(f32[16,8,128]{2,1,0:T(8,128)S(1)} %get-tuple-element.41), channel_id=1, replica_groups=mesh['grp'=8,'z'=16,'x'=4] {'z'}, dimensions={0} | all-to-all | bytes 131072 | tf_op jit(solution)/shard_map/all_to_all | solution.py:510
  87.0 0.1 shard_map.73
  87.1 12.6 %all_to_all.17.gathered = f32[32,8,128]{2,1,0:T(8,128)S(1)} all-to-all(f32[32,8,128]{2,1,0:T(8,128)S(1)} %shard_map.73), channel_id=1, replica_groups=mesh['grp'=8,'z'=16,'x'=4] {'grp','x'}, dimensions={0} | all-to-all | bytes 262144 | tf_op jit(solution)/shard_map/all_to_all | solution.py:512
  99.7 2.6 %shard_map.74 = (f32[64,128]{1,0:T(8,128)}, f32[64,128]{1,0:T(8,128)}) custom-call(f32[32,8,128]{2,1,0:T(8,128)S(1)} %all_to_all.17.gathered, f32[6,2,192,128]{3,2,1,0:T(8,128)S(1)} %get-tuple-element.32.co0, f32[6,2,96,128]{3,2,1,0:T(8,128)S(1)} %get-tuple-element.33.co1, f32[6,2,48,128]{3,2,1,0:T(8,128)S(1)} %get-tuple-element.34.co2, ...), custom_call_target="tpu_custom_call" | custom-call | tf_op jit(solution)/shard_map/pallas_call | solution.py:144
  (1 shorter events, 0.0 us)
Async XLA Ops:
  0.6 0.8 copy-start
  1.4 0.8 copy-start.1
  2.1 0.8 copy-start.2
  2.9 0.8 copy-start.3
  3.7 0.8 copy-start.4
  4.5 5.3 %collective-permute-start = (f32[2,64,128]{2,1,0:T(8,128)S(1)}, f32[2,64,128]{2,1,0:T(8,128)S(1)}, u32[]{:S(2)}, u32[]{:S(2)}) collective-permute-start(f32[2,64,128]{2,1,0:T(8,128)S(1)} %get-tuple-element.29), channel_id=1, source_target_pairs={{0,1},{1,2},{2,3},{3,4},{4,5},{5,6},{6,7},{7,8},{8,9},{9,10},{10,1... | collective-permute-start | bytes 196616 | tf_op jit(solution)/shard_map/ppermute | solution.py:434
  8.5 5.0 %collective-permute-start.1 = (f32[2,64,128]{2,1,0:T(8,128)S(1)}, f32[2,64,128]{2,1,0:T(8,128)S(1)}, u32[]{:S(2)}, u32[]{:S(2)}) collective-permute-start(f32[2,64,128]{2,1,0:T(8,128)S(1)} %get-tuple-element.30), channel_id=1, source_target_pairs={{1,0},{2,1},{3,2},{4,3},{5,4},{6,5},{7,6},{8,7},{9,8},{10,9},{11,1... | collective-permute-start | bytes 196616 | tf_op jit(solution)/shard_map/ppermute | solution.py:435
  13.6 9.2 %collective-permute-start.3 = (f32[8,64,128]{2,1,0:T(8,128)S(1)}, f32[8,64,128]{2,1,0:T(8,128)S(1)}, u32[]{:S(2)}, u32[]{:S(2)}) collective-permute-start(f32[8,64,128]{2,1,0:T(8,128)S(1)} %shard_map.69.own), channel_id=1, source_target_pairs={{64,0},{128,64},{192,128},{256,192},{320,256},{384,320},{448,384},... | collective-permute-start | bytes 786440 | tf_op jit(solution)/shard_map/ppermute | solution.py:438
  20.9 5.2 %collective-permute-start.2 = (f32[8,64,128]{2,1,0:T(8,128)S(1)}, f32[8,64,128]{2,1,0:T(8,128)S(1)}, u32[]{:S(2)}, u32[]{:S(2)}) collective-permute-start(f32[8,64,128]{2,1,0:T(8,128)S(1)} %shard_map.69.own), channel_id=1, source_target_pairs={{0,64},{64,128},{128,192},{192,256},{256,320},{320,384},{384,448},... | collective-permute-start | bytes 786440 | tf_op jit(solution)/shard_map/ppermute | solution.py:437
  27.6 5.3 %collective-permute-start.5 = (f32[8,128]{1,0:T(8,128)S(1)}, f32[8,128]{1,0:T(8,128)S(1)}, u32[]{:S(2)}, u32[]{:S(2)}) collective-permute-start(f32[8,128]{1,0:T(8,128)S(1)} %get-tuple-element.31.own), channel_id=1, source_target_pairs={{1,0},{2,1},{3,2},{4,3},{5,4},{6,5},{7,6},{8,7},{9,8},{10,9},{11,1... | collective-permute-start | bytes 12296 | tf_op jit(solution)/shard_map/ppermute | solution.py:470
  28.9 4.7 %collective-permute-start.4 = (f32[8,128]{1,0:T(8,128)S(1)}, f32[8,128]{1,0:T(8,128)S(1)}, u32[]{:S(2)}, u32[]{:S(2)}) collective-permute-start(f32[8,128]{1,0:T(8,128)S(1)} %get-tuple-element.31.own), channel_id=1, source_target_pairs={{0,1},{1,2},{2,3},{3,4},{4,5},{5,6},{6,7},{7,8},{8,9},{9,10},{10,1... | collective-permute-start | bytes 12296 | tf_op jit(solution)/shard_map/ppermute | solution.py:469

commit v2 on v1

--- a/solution.py
+++ b/solution.py
@@ -51,11 +51,6 @@
 
 def chunks(low, high, size=CHUNK):
     return [(a, min(size, high - a)) for a in range(low, high, size)]
-
-
-def clear(*refs):
-    for ref in refs:
-        ref[...] = jnp.zeros(ref.shape, F32)
 
 
 def operate(v_ref, co, a, n, step):
@@ -131,6 +126,15 @@
         put(co, a, RELAX / jnp.where(d > 0, d, 1.0), RATE)
 
 
+STATE = (208, 112, 64, 96, 48, 192)
+STATE_ROWS = sum(STATE)
+
+
+def state_of(ref):
+    starts = [sum(STATE[:k]) for k in range(6)]
+    return [ref.at[:, pl.ds(start, count), :] for start, count in zip(starts, STATE)]
+
+
 def field(*shape):
     return jax.ShapeDtypeStruct(shape, F32)
 
@@ -139,19 +143,27 @@
     return pltpu.VMEM(shape, F32)
 
 
-def call(body, outs, scratches, *args):
+def call(body, outs, scratches, *args, at=pltpu.VMEM, cycles=1000, room=12):
     vmem = pl.BlockSpec(memory_space=pltpu.VMEM)
     return pl.pallas_call(
         body,
         out_shape=outs,
-        in_specs=[vmem] * len(args),
+        in_specs=[pl.BlockSpec(memory_space=at)] * len(args),
         out_specs=jax.tree.map(lambda _: vmem, outs),
         scratch_shapes=scratches,
-        compiler_params=pltpu.CompilerParams(vmem_limit_bytes=28 * 1024 * 1024),
+        cost_estimate=pl.CostEstimate(flops=2000 * cycles, bytes_accessed=2000 * cycles, transcendentals=0),
+        compiler_params=pltpu.CompilerParams(vmem_limit_bytes=room * 1024 * 1024),
     )(*args)
 
 
-def prepare(right, previous, east, south, mask, own, to_east, to_west):
+def prepare(*refs):
+    sources, (own, to_east, to_west), temps, arrived = refs[:5], refs[5:8], refs[8:13], refs[13]
+    copies = [pltpu.make_async_copy(sources[k], temps[k], arrived.at[k]) for k in range(5)]
+    for copy in copies:
+        copy.start()
+    for copy in copies:
+        copy.wait()
+    right, previous, east, south, mask = temps
     wet = mask[...] > 0
     own[0] = jnp.where(wet, east[...], 0.0)
     own[1] = jnp.where(wet, south[...], 0.0)
@@ -187,9 +199,9 @@
     restrict(rest[2], b3_ref, l3, h3, 4)
 
 
-def first_leg(own, up, down, co0, co1, co2, b0, b1, b2, v0, v1, v2, packed, *temps):
-    wet_ref, south_ref, t0, t1, t2, r0, r1, r2, b3, co3 = temps
-    clear(wet_ref, south_ref, t0, t1, t2, v0, v1, v2)
+def first_leg(own, up, down, co0, co1, co2, state, co3, packed, *temps):
+    v0, v1, v2, b1, b2, b0 = state_of(state)
+    wet_ref, south_ref, t0, t1, t2, r0, r1, r2, b3 = temps
     parts = (up, own, down)
 
     def window(k, a, n):
@@ -217,6 +229,7 @@
     coarsen(co1, co2, 48, 2)
     set_rate(co2, 48)
     coarsen(co2, co3, 24, 4)
+    set_rate(co3, 24)
     sweep(v0, t0, co0, b0, 0, 192, 1)
     sweep(t0, v0, co0, b0, 0, 192, 1)
     residual(v0, r0, co0, b0, 0, 192, 1)
@@ -237,11 +250,47 @@
     packed[...] = out
 
 
-def fan_row(west, own, east, out):
-    for g in range(out.shape[0]):
-        out[g, 0] = west[...]
-        out[g, 1] = own[...]
-        out[g, 2] = east[...]
+def fan(own, crossed, out):
+    for k in range(out.shape[0]):
+        out[k, 0] = own[...]
+        out[k, 1] = crossed[...]
+
+
+def ascend(coarse, bases, sources, to, temp, co):
+    ranges = ((32, 160), (8, 88), (0, 48))
+    for level in (2, 1, 0):
+        low, high = ranges[level]
+        step = 1 << level
+        prolong(coarse, bases[level], to[level], low, high)
+        sweep(to[level], temp[level], co[level], sources[level], low, high, step)
+        sweep(temp[level], to[level], co[level], sources[level], low, high, step)
+        coarse = to[level]
+
+
+def second_descent(start, source, kept, rest, temp, co):
+    v0, v1, v2, b1, b2, b3 = kept
+    sweep(start, temp[0], co[0], source, 32, 160, 1)
+    sweep(temp[0], v0, co[0], source, 32, 160, 1)
+    residual(v0, rest[0], co[0], source, 32, 160, 1)
+    descend(v1, v2, b1, b2, b3, co, rest, temp, ((32, 160), (16, 80), (8, 40), (16, 32)))
+
+
+def response(co0, co1, co2, co3, state, packed, *temps):
+    v0, v1, v2, b1, b2, _ = state_of(state)
+    t0, s0, t1, s1, t2, s2, v3, s3, r0, r1, r2, b3 = temps
+    put(v3, PAD, jnp.ones((24, 256), F32))
+    sweep(v3, s3, co3, None, 0, 24, 8)
+    sweep(s3, v3, co3, None, 0, 24, 8)
+    none, co = (None, None, None), (co0, co1, co2)
+    ascend(v3, none, none, (t0, t1, t2), (s0, s1, s2), co)
+    second_descent(t0, None, (v0, v1, v2, b1, b2, b3), (r0, r1, r2), (s0, s1, s2), co)
+    packed[...] = b3[0, 8:16, :]
+
+
+def neighbours():
+    group, x = lax.axis_index("grp"), lax.axis_index("x")
+    inner_west, inner_east = x > 0, x < 3
+    return group, x, inner_west, inner_east, jnp.where(inner_west, x - 1, 3), jnp.where(inner_east, x + 1, 0)
 
 
 def spread(x, slot):
@@ -273,17 +322,18 @@
     sweep(s3, v3, co3, b3, 0, 40, 8)
 
 
-def second_leg(gathered, co0, co1, co2, b0, b1, b2, v0, v1, v2, *others):
-    (v0a, v0b, v1a, v1b, v2a, v2b, b1a, b1b, b2a, b2b, co3, co4, packed, *temps) = others
-    (t0, s0, u0, t1, s1, u1, t2, s2, u2, r0, r1, r2, e3, u3, bn, b3, b4, v3, s3, w3, v4, s4, r3, south_ref) = temps
-    clear(t0, s0, u0, t1, s1, u1, t2, s2, u2, e3, u3, v3, s3, w3, v4, s4, r3, south_ref, co4)
-    clear(v0a, v0b, v1a, v1b, v2a, v2b)
-    group = lax.axis_index("grp")
+def second_leg(gathered, responded, co0, co1, co2, before, co3, co4, after, packed, *temps):
+    v0, v1, v2, b1, b2, b0 = state_of(before)
+    v0a, v1a, v2a, b1a, b2a, _ = state_of(after)
+    (t0, s0, t1, s1, t2, s2, r0, r1, r2, e3, bn, b3, b4, v3, s3, w3, v4, s4, r3, south_ref) = temps
+    group, own, inner_west, inner_east, at_west, at_east = neighbours()
+    at_west = 2 * at_west + jnp.where(inner_west, 0, 1)
+    at_east = 2 * at_east + jnp.where(inner_east, 0, 1)
     for t in range(5):
         at = group + (t - 2)
         valid = jnp.logical_and(at >= 0, at < 8).astype(F32)
-        at = jnp.clip(at, 0, 7)
-        x = jnp.concatenate([gathered[at, k] for k in range(3)], axis=1) * valid
+        at = 8 * jnp.clip(at, 0, 7)
+        x = jnp.concatenate([gathered[at + k] for k in (at_west, 2 * own, at_east)], axis=1) * valid
         row = 8 * t
         put(b3, row, spread(x, 0))
         put(co3, row, spread(x, 1), MASS)
@@ -310,39 +360,17 @@
 
     solve_coarse(b3, b4, co3, co4, v3, s3, v4, s4, r3, None)
     inner_part(v3, e3)
-    put(v3, PAD, jnp.ones((40, 384), F32))
-    sweep(v3, s3, co3, None, 0, 40, 8)
-    sweep(s3, v3, co3, None, 0, 40, 8)
-    inner_part(v3, u3)
-    for base, coarse, b_ref, level in ((v2, e3, b2, 0), (None, u3, None, 1)):
-        e2, e1, e0 = (t2, t1, t0) if level == 0 else (u2, u1, u0)
-        prolong(coarse, base, e2, 0, 48)
-        sweep(e2, s2, co2, b_ref, 0, 48, 4)
-        sweep(s2, e2, co2, b_ref, 0, 48, 4)
-        prolong(e2, None if base is None else v1, e1, 8, 88)
-        sweep(e1, s1, co1, None if base is None else b1, 8, 88, 2)
-        sweep(s1, e1, co1, None if base is None else b1, 8, 88, 2)
-        prolong(e1, None if base is None else v0, e0, 32, 160)
-        sweep(e0, s0, co0, None if base is None else b0, 32, 160, 1)
-        sweep(s0, e0, co0, None if base is None else b0, 32, 160, 1)
-
-    source = b3[1, 16:24, :]
+    co = (co0, co1, co2)
+    ascend(e3, (v0, v1, v2), (b0, b1, b2), (t0, t1, t2), (s0, s1, s2), co)
+    second_descent(t0, b0, (v0a, v1a, v2a, b1a, b2a, bn), (r0, r1, r2), (s0, s1, s2), co)
+    result = bn[0, 8:16, :]
+    place = lanes((8, 128))
+    slot = place & 7
+    out = jnp.where(slot == 0, result, jnp.where(slot == 1, responded[...], 0.0))
     mass = co3[MASS, 1, 16:24, :]
-    results = []
-    for start, b_ref, x0, x1, x2, y1, y2 in ((t0, b0, v0a, v1a, v2a, b1a, b2a), (u0, None, v0b, v1b, v2b, b1b, b2b)):
-        clear(s0, s1, s2)
-        sweep(start, s0, co0, b_ref, 32, 160, 1)
-        sweep(s0, x0, co0, b_ref, 32, 160, 1)
-        residual(x0, r0, co0, b_ref, 32, 160, 1)
-        descend(
-            x1, x2, y1, y2, bn, (co0, co1, co2), (r0, r1, r2), (s0, s1, s2), ((32, 160), (16, 80), (8, 40), (16, 32))
-        )
-        results.append(bn[0, 8:16, :])
-    place = lanes((8, 128))
-    out = jnp.where((place & 7) == 0, results[0], jnp.where((place & 7) == 1, results[1], 0.0))
-    sums = (mass, weight * source, weight * results[0], weight * results[1])
+    sums = (mass, weight * b3[1, 16:24, :], weight * result, weight * responded[...])
     for k, value in enumerate(sums):
-        once = jnp.where((place & 7) == 0, value, 0.0)
+        once = jnp.where(slot == 0, value, 0.0)
         total = jnp.sum(jnp.sum(once, axis=0, keepdims=True), axis=1, keepdims=True)
         out = jnp.where(place == 8 * k + 6, total, out)
     for z in range(packed.shape[0]):
@@ -365,10 +393,12 @@
         out[k] = value
 
 
-def third_leg(gathered, co0, co1, co2, b0, v0a, v0b, v1a, v1b, v2a, v2b, b1a, b1b, b2a, b2b, co3, co4, *others):
+def third_leg(gathered, co0, co1, co2, before, co3, co4, after, beside, *others):
+    b0 = state_of(before)[5]
+    v0a, v1a, v2a, b1a, b2a, _ = state_of(after)
+    v0b, v1b, v2b, b1b, b2b, _ = state_of(beside)
     (surface, rest, *temps) = others
     (t0, s0, c0, t1, s1, c1, d1, t2, s2, c2, d2, e3, b3, b4, v3, s3, v4, s4, r3) = temps
-    clear(t0, s0, c0, t1, s1, c1, t2, s2, c2, e3, v3, s3, v4, s4, r3)
     total = gathered[0]
     for k in range(1, gathered.shape[0]):
         total = total + gathered[k]
@@ -379,10 +409,7 @@
     shift1 = RELAX * sum1 / mass
     shift2 = RELAX * (sum2a + shift1 * sum2b) / mass
 
-    group, x = lax.axis_index("grp"), lax.axis_index("x")
-    inner_west, inner_east = x > 0, x < 3
-    at_west = jnp.where(inner_west, x - 1, 3)
-    at_east = jnp.where(inner_east, x + 1, 0)
+    group, x, inner_west, inner_east, at_west, at_east = neighbours()
     for t in range(5):
         g = 4 * jnp.clip(group + (t - 2), 0, 7)
         w, o, e = gathered[g + at_west], gathered[g + x], gathered[g + at_east]
@@ -424,12 +451,14 @@
     own, to_east, to_west = call(
         prepare,
         (field(4, 64, 128), field(2, 64, 128), field(2, 64, 128)),
-        [],
+        [*[scratch(64, 128)] * 4, pltpu.VMEM((64, 128), jnp.int32), pltpu.SemaphoreType.DMA((5,))],
         right_side,
         previous,
         east_face,
         south_face,
         wet_mask,
+        at=pltpu.HBM,
+        room=60,
     )
     west = lax.ppermute(to_east, dev, to_next)
     east = lax.ppermute(to_west, dev, to_last)
@@ -446,65 +475,47 @@
     def as_scratch(*fields):
         return [scratch(*f.shape) for f in fields]
 
-    co = [field(6, 2, count, 128) for count in (192, 96, 48)]
-    *kept, packed = call(
+    co = [field(6, 2, count, 128) for count in (192, 96, 48, 24)]
+    fine = [shifted(count) for count in (192, 96, 48)]
+    sources = [rows(count) for count in (192, 96, 48)]
+    state = rows(STATE_ROWS)
+    *kept, near, packed = call(
         first_leg,
-        (*co, rows(192), rows(96), rows(48), shifted(192), shifted(96), shifted(48), field(8, 128)),
-        as_scratch(
-            shifted(192),
-            shifted(192),
-            shifted(192),
-            shifted(96),
-            shifted(48),
-            rows(192),
-            rows(96),
-            rows(48),
-            rows(24),
-            field(6, 2, 24, 128),
-        ),
+        (*co[:3], state, co[3], field(8, 128)),
+        as_scratch(fine[0], fine[0], *fine, *sources, rows(24)),
         own,
         up,
         down,
     )
-    west = lax.ppermute(packed, dev, to_next)
-    east = lax.ppermute(packed, dev, to_last)
-    gathered = call(fan_row, field(8, 3, 8, 128), [], west, packed, east)
-    gathered = lax.all_to_all(gathered, "grp", 0, 0, tiled=True)
-    wide = [shifted(40, 3), shifted(40, 3), shifted(40, 3), shifted(24, 3), shifted(24, 3)]
+    crossings = [(4 * z + 3, 4 * z + 7) for z in range(15)] + [(4 * z + 4, 4 * z) for z in range(15)]
+    crossed = lax.ppermute(packed, dev, crossings)
+    beside, responded = call(
+        response,
+        (state, field(8, 128)),
+        as_scratch(*[f for f in fine for _ in range(2)], shifted(24), shifted(24), *sources, rows(24)),
+        *kept[:3],
+        near,
+        cycles=3000,
+    )
+    gathered = call(fan, field(32, 2, 8, 128), [], packed, crossed)
+    gathered = lax.all_to_all(gathered, ("grp", "x"), 0, 0, tiled=True).reshape(64, 8, 128)
+    coarse = [shifted(40, 3), shifted(40, 3), shifted(40, 3), shifted(24, 3), shifted(24, 3)]
     *second, packed = call(
         second_leg,
-        (
-            shifted(192),
-            shifted(192),
-            shifted(96),
-            shifted(96),
-            shifted(48),
-            shifted(48),
-            rows(96),
-            rows(96),
-            rows(48),
-            rows(48),
-            field(6, 3, 40, 128),
-            field(6, 3, 24, 128),
-            field(16, 8, 128),
-        ),
+        (field(6, 3, 40, 128), field(6, 3, 24, 128), state, field(16, 8, 128)),
         as_scratch(
-            *[shifted(192)] * 3,
-            *[shifted(96)] * 3,
-            *[shifted(48)] * 3,
-            rows(192),
-            rows(96),
-            rows(48),
-            shifted(24),
+            *[f for f in fine for _ in range(2)],
+            *sources,
             shifted(24),
             rows(24),
             rows(40, 3),
             rows(24, 3),
-            *wide,
+            *coarse,
             rows(48, 3),
             shifted(40, 3),
         ),
         gathered,
+        responded,
         *kept,
     )
     gathered = lax.all_to_all(packed, "z", 0, 0, tiled=True)
@@ -529,8 +540,9 @@
             rows(48, 3),
         ),
         gathered,
-        *kept[:4],
+        *kept,
         *second,
+        beside,
     )
     return surface, rest
 

time: 103 us -> 96.5 us (0.937)
  blocking collectives: 59.3 us -> 40.2 us
  waiting for transfers between devices: 7.73 us -> 16.6 us
  starting transfers between devices: 19.7 us -> 25 us
  local copies, waits for them, and re-layouts: 3.78 us -> 1.78 us
    all_to_all x1 -> x0, blocking collectives: 10 us -> none  [shards(): gathered = lax.all_to_all(gathered, 'grp', 0, 0, tiled=True)]
    all_to_all x1, blocking collectives: 36.6 us -> 27.2 us  [shards(): gathered = lax.all_to_all(packed, 'z', 0, 0, tiled=True)]
    all_to_all x0 -> x1, starting transfers between devices: none -> 9.27 us  [shards(): lax.all_to_all(gathered, ('grp', 'x'), 0, 0, tiled=True).reshape(64, 8, 128)]
    all_to_all x0 -> x1, waiting for transfers between devices: none -> 6.34 us  [shards(): lax.all_to_all(gathered, ('grp', 'x'), 0, 0, tiled=True).reshape(64, 8, 128)]
    ppermute x2 -> x1, starting transfers between devices: 5.29 us -> 1.3 us  [shards(): crossed = lax.ppermute(packed, dev, crossings)]
    ppermute x2 -> x1, waiting for transfers between devices: 0.73 us -> 3.05 us  [shards(): crossed = lax.ppermute(packed, dev, crossings)]
    unnamed x10 -> x6, local copies, waits for them, and re-layouts: 3.78 us -> 1.78 us
    pallas_call x7 -> x8, Pallas kernels: 11.1 us -> 11.7 us  [call(): pl.pallas_call(body, out_shape=outs, in_specs=[pl.BlockSpec(memory_space=...]
  transfers between devices with their start and end apart: 6 -> 6, of which waited for: 3 -> 5; matrix products, arithmetic and copies ran while one was open for 0% -> 0% of each run, Pallas kernels for 0% -> 2%
where the time goes in v2:
time: 96.5 us; the launch traced here: 96 us
  blocking collectives  40.2 us (42%)
  starting transfers between devices  25 us (26%)
  waiting for transfers between devices  16.6 us (17%)
  Pallas kernels  11.7 us (12%)
  local copies, waits for them, and re-layouts  1.78 us (2%)
    all_to_all x1, blocking collectives, shards(): gathered = lax.all_to_all(packed, 'z', 0, 0, tiled=True)  27.2 us
    all_to_all x1, blocking collectives, shards(): gathered = lax.all_to_all(gathered, ('grp', 'x'), 0, 0, tiled=True)  13 us
    pallas_call x8, Pallas kernels, call(): pl.pallas_call(body, out_shape=outs, in_specs=[pl.BlockSpec(memory_space=...  11.7 us
    all_to_all x1, starting transfers between devices, shards(): lax.all_to_all(gathered, ('grp', 'x'), 0, 0, tiled=True).reshape(64, 8, 128)  9.27 us
    ppermute x1, starting transfers between devices, shards(): down = lax.ppermute(own, 'grp', to_last[:7])  7.28 us
    all_to_all x1, waiting for transfers between devices, shards(): lax.all_to_all(gathered, ('grp', 'x'), 0, 0, tiled=True).reshape(64, 8, 128)  6.34 us
    ppermute x1, starting transfers between devices, shards(): west = lax.ppermute(to_east, dev, to_next)  3.95 us
    ppermute x1, waiting for transfers between devices, shards(): east = lax.ppermute(to_west, dev, to_last)  3.59 us
  transfers between devices with their start and end apart: 6, of which 5 were waited for; matrix products, arithmetic and copies ran while one was open for 0% of the time, Pallas kernels for 2%

profile of v2, /device:TPU:1, one launch (start us, length us, event | category | flops | bytes accessed | tf_op | source)
XLA Modules:
  0.0 96.0 jit_solution(1515878855228858383)
XLA Ops:
  0.6 1.6 %shard_map.68 = (f32[4,64,128]{2,1,0:T(8,128)}, f32[2,64,128]{2,1,0:T(8,128)}, f32[2,64,128]{2,1,0:T(8,128)}) custom-call(f32[64,128]{1,0:T(8,128)} %refs_0_.1, f32[64,128]{1,0:T(8,128)} %refs_1_.1, f32[64,128]{1,0:T(8,128)} %refs_2_.1, f32[64,128]{1,0:T(8,128)} %refs_3_.1, s32[64,128]{1,0:T(8,128)} %refs_4_.1), custom_call_target="tpu_custom_call" | custom-call | flops 2000000 | bytes 2000000 | tf_op jit(solution)/shard_map/pallas_call | solution.py:148
  2.2 3.9 %collective-permute-start = (f32[2,64,128]{2,1,0:T(8,128)}, f32[2,64,128]{2,1,0:T(8,128)S(1)}, u32[]{:S(2)}, u32[]{:S(2)}) collective-permute-start(f32[2,64,128]{2,1,0:T(8,128)} %get-tuple-element.18), channel_id=1, source_target_pairs={{0,1},{1,2},{2,3},{3,4},{4,5},{5,6},{6,7},{7,8},{8,9},{9,10},{10,1... | collective-permute-start | bytes 196616 | tf_op jit(solution)/shard_map/ppermute | solution.py:463
  6.2 1.3 %collective-permute-start.1 = (f32[2,64,128]{2,1,0:T(8,128)}, f32[2,64,128]{2,1,0:T(8,128)S(1)}, u32[]{:S(2)}, u32[]{:S(2)}) collective-permute-start(f32[2,64,128]{2,1,0:T(8,128)} %get-tuple-element.19), channel_id=1, source_target_pairs={{1,0},{2,1},{3,2},{4,3},{5,4},{6,5},{7,6},{8,7},{9,8},{10,9},{11,1... | collective-permute-start | bytes 196616 | tf_op jit(solution)/shard_map/ppermute | solution.py:464
  7.5 0.3 collective-permute-done.west
  7.8 3.6 %collective-permute-done.1.east = f32[2,64,128]{2,1,0:T(8,128)S(1)} collective-permute-done((f32[2,64,128]{2,1,0:T(8,128)}, f32[2,64,128]{2,1,0:T(8,128)S(1)}, u32[]{:S(2)}, u32[]{:S(2)}) %collective-permute-start.1) | collective-permute-done | bytes 65568 | tf_op jit(solution)/shard_map/ppermute | solution.py:464
  11.4 0.0 copy-start.2
  11.4 0.9 copy-done.2
  12.3 0.1 shard_map.69.own
  12.4 7.3 %collective-permute-start.3 = (f32[8,64,128]{2,1,0:T(8,128)S(1)}, f32[8,64,128]{2,1,0:T(8,128)S(1)}, u32[]{:S(2)}, u32[]{:S(2)}) collective-permute-start(f32[8,64,128]{2,1,0:T(8,128)S(1)} %shard_map.69.own), channel_id=1, source_target_pairs={{64,0},{128,64},{192,128},{256,192},{320,256},{384,320},{448,384},... | collective-permute-start | bytes 786440 | tf_op jit(solution)/shard_map/ppermute | solution.py:467
  19.7 1.9 %collective-permute-start.2 = (f32[8,64,128]{2,1,0:T(8,128)S(1)}, f32[8,64,128]{2,1,0:T(8,128)S(1)}, u32[]{:S(2)}, u32[]{:S(2)}) collective-permute-start(f32[8,64,128]{2,1,0:T(8,128)S(1)} %shard_map.69.own), channel_id=1, source_target_pairs={{0,64},{64,128},{128,192},{192,256},{256,320},{320,384},{384,448},... | collective-permute-start | bytes 786440 | tf_op jit(solution)/shard_map/ppermute | solution.py:466
  21.6 0.0 collective-permute-done.3.down
  21.7 3.3 %collective-permute-done.2.up = f32[8,64,128]{2,1,0:T(8,128)S(1)} collective-permute-done((f32[8,64,128]{2,1,0:T(8,128)S(1)}, f32[8,64,128]{2,1,0:T(8,128)S(1)}, u32[]{:S(2)}, u32[]{:S(2)}) %collective-permute-start.2) | collective-permute-done | bytes 262176 | tf_op jit(solution)/shard_map/ppermute | solution.py:466
  24.9 1.5 %shard_map.70 = (f32[6,2,192,128]{3,2,1,0:T(8,128)S(1)}, f32[6,2,96,128]{3,2,1,0:T(8,128)S(1)}, f32[6,2,48,128]{3,2,1,0:T(8,128)S(1)}, f32[2,720,128]{2,1,0:T(8,...) custom-call(f32[8,64,128]{2,1,0:T(8,128)S(1)} %shard_map.69.own, ...), custom_call_target="tpu_custom_call" | custom-call | flops 2000000 | bytes 2000000 | tf_op jit(solution)/shard_map/pallas_call | solution.py:148
  26.5 1.3 %collective-permute-start.4 = (f32[8,128]{1,0:T(8,128)S(1)}, f32[8,128]{1,0:T(8,128)S(1)}, u32[]{:S(2)}, u32[]{:S(2)}) collective-permute-start(f32[8,128]{1,0:T(8,128)S(1)} %get-tuple-element.20.own), channel_id=1, source_target_pairs={{3,7},{7,11},{11,15},{15,19},{19,23},{23,27},{27,31},{31,35},{35,3... | collective-permute-start | bytes 12296 | tf_op jit(solution)/shard_map/ppermute | solution.py:491
  27.8 3.1 %collective-permute-done.4.crossed = f32[8,128]{1,0:T(8,128)S(1)} collective-permute-done((f32[8,128]{1,0:T(8,128)S(1)}, f32[8,128]{1,0:T(8,128)S(1)}, u32[]{:S(2)}, u32[]{:S(2)}) %collective-permute-start.4) | collective-permute-done | bytes 4128 | tf_op jit(solution)/shard_map/ppermute | solution.py:491
  30.8 0.7 shard_map.71
  31.5 9.3 %all-to-all-start = ((f32[32,2,8,128]{3,2,1,0:T(8,128)}), f32[32,2,8,128]{3,2,1,0:T(8,128)S(1)}, u32[]{:S(2)}, u32[]{:S(2)}) async-start(f32[32,2,8,128]{3,2,1,0:T(8,128)} %shard_map.71), calls=%async_computation | async-start | bytes 524288 | tf_op jit(solution)/shard_map/all_to_all | solution.py:501
  40.8 1.7 %shard_map.72 = (f32[2,720,128]{2,1,0:T(8,128)S(1)}, f32[8,128]{1,0:T(8,128)S(1)}) custom-call(f32[6,2,192,128]{3,2,1,0:T(8,128)S(1)} %get-tuple-element.21.co0, f32[6,2,96,128]{3,2,1,0:T(8,128)S(1)} %get-tuple-element.22.co1, f32[6,2,48,128]{3,2,1,0:T(8,128)S(1)} %get-tuple-element.23.co2, f32[6,2,24,128]{3,2,1,0:T(8,128)S(1)} %get-tuple-element.24.co3), custom_call_target="tpu_custom_call" | custom-call | flops 6000000 | bytes 6000000 | tf_op jit(solution)/shard_map/pallas_call | solution.py:148
  42.5 0.0 copy-start
  42.5 0.9 copy-done
  43.4 6.3 %all-to-all-done = f32[32,2,8,128]{3,2,1,0:T(8,128)S(1)} async-done(((f32[32,2,8,128]{3,2,1,0:T(8,128)}), f32[32,2,8,128]{3,2,1,0:T(8,128)S(1)}, u32[]{:S(2)}, u32[]{:S(2)}) %all-to-all-start) | async-done | bytes 262176 | tf_op jit(solution)/shard_map/all_to_all | solution.py:501
  49.7 0.0 copy-start.1
  49.7 3.4 %shard_map.73 = (f32[6,3,40,128]{3,2,1,0:T(8,128)S(1)}, f32[6,3,24,128]{3,2,1,0:T(8,128)S(1)}, f32[2,720,128]{2,1,0:T(8,128)S(1)}, f32[16,8,128]{2,1,0:T(8,128)S(1)}) custom-call(f32[64,8,128]{2,1,0:T(8,128)S(1)} %bitcast.1, f32[8,128]{1,0:T(8,128)S(1)} %get-tuple-element.25.responded, f32[6,2,192,128]{3,2,1,0:T(8,128)S(1)} %get-tuple-element.21.co0, ...), custom_call_target="tpu_custom_call" | custom-call | flops 2000000 | bytes 2000000 | tf_op jit(solution)/shard_map/pallas_call | solution.py:148
  53.1 27.2 %all_to_all.15.gathered = f32[16,8,128]{2,1,0:T(8,128)S(1)} all-to-all(f32[16,8,128]{2,1,0:T(8,128)S(1)} %get-tuple-element.27), channel_id=1, replica_groups=mesh['grp'=8,'z'=16,'x'=4] {'z'}, dimensions={0} | all-to-all | bytes 131072 | tf_op jit(solution)/shard_map/all_to_all | solution.py:521
  80.3 0.1 shard_map.74
  80.4 13.0 %all_to_all.16.gathered = f32[32,8,128]{2,1,0:T(8,128)S(1)} all-to-all(f32[32,8,128]{2,1,0:T(8,128)S(1)} %shard_map.74), channel_id=1, replica_groups=mesh['grp'=8,'z'=16,'x'=4] {'grp','x'}, dimensions={0} | all-to-all | bytes 262144 | tf_op jit(solution)/shard_map/all_to_all | solution.py:523
  93.4 0.0 copy-done.1
  93.4 2.6 %shard_map.75 = (f32[64,128]{1,0:T(8,128)}, f32[64,128]{1,0:T(8,128)}) custom-call(f32[32,8,128]{2,1,0:T(8,128)S(1)} %all_to_all.16.gathered, f32[6,2,192,128]{3,2,1,0:T(8,128)S(1)} %get-tuple-element.21.co0, f32[6,2,96,128]{3,2,1,0:T(8,128)S(1)} %get-tuple-element.22.co1, f32[6,2,48,128]{3,2,1,0:T(8,128)S(1)} %get-tuple-element.23.co2, ...), custom_call_target="tpu_custom_call" | custom-call | flops 2000000 | bytes 2000000 | tf_op jit(solution)/shard_map/pallas_call | solution.py:148
Async XLA Ops:
  2.2 5.6 %collective-permute-start = (f32[2,64,128]{2,1,0:T(8,128)}, f32[2,64,128]{2,1,0:T(8,128)S(1)}, u32[]{:S(2)}, u32[]{:S(2)}) collective-permute-start(f32[2,64,128]{2,1,0:T(8,128)} %get-tuple-element.18), channel_id=1, source_target_pairs={{0,1},{1,2},{2,3},{3,4},{4,5},{5,6},{6,7},{7,8},{8,9},{9,10},{10,1... | collective-permute-start | bytes 196616 | tf_op jit(solution)/shard_map/ppermute | solution.py:463
  6.2 5.2 %collective-permute-start.1 = (f32[2,64,128]{2,1,0:T(8,128)}, f32[2,64,128]{2,1,0:T(8,128)S(1)}, u32[]{:S(2)}, u32[]{:S(2)}) collective-permute-start(f32[2,64,128]{2,1,0:T(8,128)} %get-tuple-element.19), channel_id=1, source_target_pairs={{1,0},{2,1},{3,2},{4,3},{5,4},{6,5},{7,6},{8,7},{9,8},{10,9},{11,1... | collective-permute-start | bytes 196616 | tf_op jit(solution)/shard_map/ppermute | solution.py:464
  11.4 0.9 copy-start.2
  12.4 9.2 %collective-permute-start.3 = (f32[8,64,128]{2,1,0:T(8,128)S(1)}, f32[8,64,128]{2,1,0:T(8,128)S(1)}, u32[]{:S(2)}, u32[]{:S(2)}) collective-permute-start(f32[8,64,128]{2,1,0:T(8,128)S(1)} %shard_map.69.own), channel_id=1, source_target_pairs={{64,0},{128,64},{192,128},{256,192},{320,256},{384,320},{448,384},... | collective-permute-start | bytes 786440 | tf_op jit(solution)/shard_map/ppermute | solution.py:467
  19.7 5.2 %collective-permute-start.2 = (f32[8,64,128]{2,1,0:T(8,128)S(1)}, f32[8,64,128]{2,1,0:T(8,128)S(1)}, u32[]{:S(2)}, u32[]{:S(2)}) collective-permute-start(f32[8,64,128]{2,1,0:T(8,128)S(1)} %shard_map.69.own), channel_id=1, source_target_pairs={{0,64},{64,128},{128,192},{192,256},{256,320},{320,384},{384,448},... | collective-permute-start | bytes 786440 | tf_op jit(solution)/shard_map/ppermute | solution.py:466
  26.5 4.4 %collective-permute-start.4 = (f32[8,128]{1,0:T(8,128)S(1)}, f32[8,128]{1,0:T(8,128)S(1)}, u32[]{:S(2)}, u32[]{:S(2)}) collective-permute-start(f32[8,128]{1,0:T(8,128)S(1)} %get-tuple-element.20.own), channel_id=1, source_target_pairs={{3,7},{7,11},{11,15},{15,19},{19,23},{23,27},{27,31},{31,35},{35,3... | collective-permute-start | bytes 12296 | tf_op jit(solution)/shard_map/ppermute | solution.py:491
  31.5 18.2 %all-to-all-start = ((f32[32,2,8,128]{3,2,1,0:T(8,128)}), f32[32,2,8,128]{3,2,1,0:T(8,128)S(1)}, u32[]{:S(2)}, u32[]{:S(2)}) async-start(f32[32,2,8,128]{3,2,1,0:T(8,128)} %shard_map.71), calls=%async_computation | async-start | bytes 524288 | tf_op jit(solution)/shard_map/all_to_all | solution.py:501
  42.5 0.9 copy-start
  49.7 43.7 %copy-start.1 = (f32[2,720,128]{2,1,0:T(8,128)S(1)}, f32[2,720,128]{2,1,0:T(8,128)}, u32[]{:S(2)}) copy-start(f32[2,720,128]{2,1,0:T(8,128)} %copy-done) | copy-start | bytes 2211844

commit v3 on v2

--- a/solution.py
+++ b/solution.py
@@ -149,7 +149,7 @@
         body,
         out_shape=outs,
         in_specs=[pl.BlockSpec(memory_space=at)] * len(args),
-        out_specs=jax.tree.map(lambda _: vmem, outs),
+        out_specs=[vmem] * len(outs) if isinstance(outs, tuple) else vmem,
         scratch_shapes=scratches,
         cost_estimate=pl.CostEstimate(flops=2000 * cycles, bytes_accessed=2000 * cycles, transcendentals=0),
         compiler_params=pltpu.CompilerParams(vmem_limit_bytes=room * 1024 * 1024),
@@ -157,7 +157,7 @@
 
 
 def prepare(*refs):
-    sources, (own, to_east, to_west), temps, arrived = refs[:5], refs[5:8], refs[8:13], refs[13]
+    sources, (own, first, second), temps, arrived = refs[:5], refs[5:8], refs[8:13], refs[13]
     copies = [pltpu.make_async_copy(sources[k], temps[k], arrived.at[k]) for k in range(5)]
     for copy in copies:
         copy.start()
@@ -170,16 +170,20 @@
     own[2] = jnp.where(wet, right[...], previous[...])
     own[3] = previous[...]
     low = lanes((64, 128)) < 64
+    even = lax.rem(lax.axis_index("x"), 2) == 0
     for k in range(2):
         a, b = own[2 * k], pltpu.roll(own[2 * k + 1], 64, 1)
-        to_east[k] = jnp.where(low, b, a)
-        to_west[k] = jnp.where(low, a, b)
-
-
-def widen(own, west, east, out):
+        to_east, to_west = jnp.where(low, b, a), jnp.where(low, a, b)
+        first[k] = jnp.where(even, to_east, to_west)
+        second[k] = jnp.where(even, to_west, to_east)
+
+
+def widen(own, first, second, out):
     low = lanes((64, 128)) < 64
+    even = lax.rem(lax.axis_index("x"), 2) == 0
     for k in range(2):
-        e, w = east[k], west[k]
+        e = jnp.where(even, first[k], second[k])
+        w = jnp.where(even, second[k], first[k])
         out[2 * k] = own[2 * k]
         out[2 * k + 1] = own[2 * k + 1]
         out[4 + 2 * k] = jnp.where(low, e, w)
@@ -199,14 +203,18 @@
     restrict(rest[2], b3_ref, l3, h3, 4)
 
 
-def first_leg(own, up, down, co0, co1, co2, state, co3, packed, *temps):
+def first_leg(own, first, second, co0, co1, co2, state, co3, packed, *temps):
     v0, v1, v2, b1, b2, b0 = state_of(state)
     wet_ref, south_ref, t0, t1, t2, r0, r1, r2, b3 = temps
-    parts = (up, own, down)
+    even = lax.rem(lax.axis_index("grp"), 2) == 0
 
     def window(k, a, n):
-        ref, o = parts[a // 64], a % 64
-        return jnp.concatenate([ref[k, o : o + n, :], ref[4 + k, o : o + n, :]], axis=1)
+        part, o = a // 64, a % 64
+        if part == 1:
+            return jnp.concatenate([own[k, o : o + n, :], own[4 + k, o : o + n, :]], axis=1)
+        up, down = (second, first) if part == 0 else (first, second)
+        halves = [jnp.where(even, up[h, o : o + n, :], down[h, o : o + n, :]) for h in (k, 4 + k)]
+        return jnp.concatenate(halves, axis=1)
 
     for a, n in chunks(0, 192):
         put(wet_ref, PAD + a, jnp.where(window(0, a, n) > 0, 1.0, 0.0))
@@ -250,9 +258,10 @@
     packed[...] = out
 
 
-def fan(own, crossed, out):
+def fan(own, crossed, responded, out):
+    full = jnp.where((lanes((8, 128)) & 7) == 5, responded[...], own[...])
     for k in range(out.shape[0]):
-        out[k, 0] = own[...]
+        out[k, 0] = full
         out[k, 1] = crossed[...]
 
 
@@ -444,13 +453,16 @@
         rest[a - 64 : a - 64 + n, :] = b0[0, a : a + n, :] - out[:, :128]
 
 
+def swaps(start, count):
+    low = range(start, count - 1, 2)
+    return [(i, i + 1) for i in low] + [(i + 1, i) for i in low]
+
+
 def shards(right_side, previous, east_face, south_face, wet_mask):
     dev = ("z", "x")
-    to_next = [(i, i + 1) for i in range(63)]
-    to_last = [(j, i) for i, j in to_next]
-    own, to_east, to_west = call(
+    own, first, second = call(
         prepare,
-        (field(4, 64, 128), field(2, 64, 128), field(2, 64, 128)),
+        (scratch(4, 64, 128), scratch(2, 64, 128), scratch(2, 64, 128)),
         [*[scratch(64, 128)] * 4, pltpu.VMEM((64, 128), jnp.int32), pltpu.SemaphoreType.DMA((5,))],
         right_side,
         previous,
@@ -460,11 +472,11 @@
         at=pltpu.HBM,
         room=60,
     )
-    west = lax.ppermute(to_east, dev, to_next)
-    east = lax.ppermute(to_west, dev, to_last)
-    own = call(widen, field(8, 64, 128), [], own, west, east)
-    up = lax.ppermute(own, "grp", to_next[:7])
-    down = lax.ppermute(own, "grp", to_last[:7])
+    first = lax.ppermute(first, dev, swaps(0, 64))
+    second = lax.ppermute(second, dev, swaps(1, 64))
+    own = call(widen, field(8, 64, 128), [], own, first, second)
+    first = lax.ppermute(own, "grp", swaps(0, 8))
+    second = lax.ppermute(own, "grp", swaps(1, 8))
 
     def rows(count, planes=2):
         return field(planes, count, 128)
@@ -484,8 +496,8 @@
         (*co[:3], state, co[3], field(8, 128)),
         as_scratch(fine[0], fine[0], *fine, *sources, rows(24)),
         own,
-        up,
-        down,
+        first,
+        second,
     )
     crossings = [(4 * z + 3, 4 * z + 7) for z in range(15)] + [(4 * z + 4, 4 * z) for z in range(15)]
     crossed = lax.ppermute(packed, dev, crossings)
@@ -497,7 +509,7 @@
         near,
         cycles=3000,
     )
-    gathered = call(fan, field(32, 2, 8, 128), [], packed, crossed)
+    gathered = call(fan, field(32, 2, 8, 128), [], packed, crossed, responded)
     gathered = lax.all_to_all(gathered, ("grp", "x"), 0, 0, tiled=True).reshape(64, 8, 128)
     coarse = [shifted(40, 3), shifted(40, 3), shifted(40, 3), shifted(24, 3), shifted(24, 3)]
     *second, packed = call(

time: 96.5 us -> 91.5 us (0.948)
  blocking collectives: 40.2 us -> 56.9 us
  waiting for transfers between devices: 16.6 us -> 7.2 us
  starting transfers between devices: 25 us -> 15.9 us
  local copies, waits for them, and re-layouts: 1.78 us -> 0 us
  Pallas kernels: 11.7 us -> 10.4 us
    all_to_all x0 -> x1, blocking collectives: none -> 16.4 us  [shards(): lax.all_to_all(gathered, ('grp', 'x'), 0, 0, tiled=True).reshape(64, 8, 128)]
    all_to_all x1 -> x0, starting transfers between devices: 9.27 us -> none  [shards(): lax.all_to_all(gathered, ('grp', 'x'), 0, 0, tiled=True).reshape(64, 8, 128)]
    all_to_all x1 -> x0, waiting for transfers between devices: 6.34 us -> none  [shards(): lax.all_to_all(gathered, ('grp', 'x'), 0, 0, tiled=True).reshape(64, 8, 128)]
    ppermute x4, waiting for transfers between devices: 7.21 us -> 2.1 us  [the longest x1 1.13 us: shards(): first = lax.ppermute(own, 'grp', swaps(0, 8))]
    ppermute x1, waiting for transfers between devices: 3.05 us -> 5.1 us  [shards(): crossed = lax.ppermute(packed, dev, crossings)]
    unnamed x6 -> x0, local copies, waits for them, and re-layouts: 1.78 us -> none
    pallas_call x8, Pallas kernels: 11.7 us -> 10.4 us  [call(): pl.pallas_call(body, out_shape=outs, in_specs=[pl.BlockSpec(memory_space=...]
  transfers between devices with their start and end apart: 6 -> 5, of which waited for: 5 -> 3; matrix products, arithmetic and copies ran while one was open for 0% -> 0% of each run, Pallas kernels for 2% -> 2%
where the time goes in v3:
time: 91.5 us; the launch traced here: 91.2 us
  blocking collectives  56.9 us (62%)
  starting transfers between devices  15.9 us (17%)
  Pallas kernels  10.4 us (11%)
  waiting for transfers between devices  7.2 us (8%)
    all_to_all x1, blocking collectives, shards(): gathered = lax.all_to_all(packed, 'z', 0, 0, tiled=True)  27.5 us
    all_to_all x1, blocking collectives, shards(): lax.all_to_all(gathered, ('grp', 'x'), 0, 0, tiled=True).reshape(64, 8, 128)  16.4 us
    all_to_all x1, blocking collectives, shards(): gathered = lax.all_to_all(gathered, ('grp', 'x'), 0, 0, tiled=True)  13 us
    pallas_call x8, Pallas kernels, call(): pl.pallas_call(body, out_shape=outs, in_specs=[pl.BlockSpec(memory_space=...  10.4 us
    ppermute x1, starting transfers between devices, shards(): second = lax.ppermute(own, 'grp', swaps(1, 8))  5.16 us
    ppermute x1, waiting for transfers between devices, shards(): crossed = lax.ppermute(packed, dev, crossings)  5.1 us
    ppermute x1, starting transfers between devices, shards(): first = lax.ppermute(own, 'grp', swaps(0, 8))  4.87 us
    ppermute x1, starting transfers between devices, shards(): first = lax.ppermute(first, dev, swaps(0, 64))  3.95 us
  transfers between devices with their start and end apart: 5, of which 3 were waited for; matrix products, arithmetic and copies ran while one was open for 0% of the time, Pallas kernels for 2%

profile of v3, /device:TPU:1, one launch (start us, length us, event | category | flops | bytes accessed | tf_op | source)
XLA Modules:
  0.0 91.2 jit_solution(607590410831525163)
XLA Ops:
  0.6 1.0 %shard_map.68 = (f32[4,64,128]{2,1,0:T(8,128)S(1)}, f32[2,64,128]{2,1,0:T(8,128)S(1)}, f32[2,64,128]{2,1,0:T(8,128)S(1)}) custom-call(f32[64,128]{1,0:T(8,128)} %refs_0_.1, f32[64,128]{1,0:T(8,128)} %refs_1_.1, f32[64,128]{1,0:T(8,128)} %refs_2_.1, f32[64,128]{1,0:T(8,128)} %refs_3_.1, s32[64,128]{1,0:T(8,128)} %refs_4_.1), custom_call_target="tpu_custom_call" | custom-call | flops 2000000 | bytes 2000000 | tf_op jit(solution)/shard_map/pallas_call | solution.py:148
  1.6 3.9 %collective-permute-start = (f32[2,64,128]{2,1,0:T(8,128)S(1)}, f32[2,64,128]{2,1,0:T(8,128)S(1)}, u32[]{:S(2)}, u32[]{:S(2)}) collective-permute-start(f32[2,64,128]{2,1,0:T(8,128)S(1)} %get-tuple-element.18), channel_id=1, source_target_pairs={{0,1},{2,3},{4,5},{6,7},{8,9},{10,11},{12,13},{14,15},{16,17},{18,... | collective-permute-start | bytes 196616 | tf_op jit(solution)/shard_map/ppermute | solution.py:475
  5.5 0.7 collective-permute-start.1
  6.2 1.0 %collective-permute-done.first = f32[2,64,128]{2,1,0:T(8,128)S(1)} collective-permute-done((f32[2,64,128]{2,1,0:T(8,128)S(1)}, f32[2,64,128]{2,1,0:T(8,128)S(1)}, u32[]{:S(2)}, u32[]{:S(2)}) %collective-permute-start) | collective-permute-done | bytes 65568 | tf_op jit(solution)/shard_map/ppermute | solution.py:475
  7.2 0.0 collective-permute-done.1.second
  7.2 0.1 shard_map.69.own
  7.3 5.2 %collective-permute-start.3 = (f32[8,64,128]{2,1,0:T(8,128)S(1)}, f32[8,64,128]{2,1,0:T(8,128)S(1)}, u32[]{:S(2)}, u32[]{:S(2)}) collective-permute-start(f32[8,64,128]{2,1,0:T(8,128)S(1)} %shard_map.69.own), channel_id=1, source_target_pairs={{64,128},{192,256},{320,384},{128,64},{256,192},{384,320},{65,129}... | collective-permute-start | bytes 786440 | tf_op jit(solution)/shard_map/ppermute | solution.py:479
  12.5 4.9 %collective-permute-start.2 = (f32[8,64,128]{2,1,0:T(8,128)S(1)}, f32[8,64,128]{2,1,0:T(8,128)S(1)}, u32[]{:S(2)}, u32[]{:S(2)}) collective-permute-start(f32[8,64,128]{2,1,0:T(8,128)S(1)} %shard_map.69.own), channel_id=1, source_target_pairs={{0,64},{128,192},{256,320},{384,448},{64,0},{192,128},{320,256},{4... | collective-permute-start | bytes 786440 | tf_op jit(solution)/shard_map/ppermute | solution.py:478
  17.3 0.0 collective-permute-done.3.second
  17.3 1.1 %collective-permute-done.2.first = f32[8,64,128]{2,1,0:T(8,128)S(1)} collective-permute-done((f32[8,64,128]{2,1,0:T(8,128)S(1)}, f32[8,64,128]{2,1,0:T(8,128)S(1)}, u32[]{:S(2)}, u32[]{:S(2)}) %collective-permute-start.2) | collective-permute-done | bytes 262176 | tf_op jit(solution)/shard_map/ppermute | solution.py:478
  18.5 1.5 %shard_map.70 = (f32[6,2,192,128]{3,2,1,0:T(8,128)S(1)}, f32[6,2,96,128]{3,2,1,0:T(8,128)S(1)}, f32[6,2,48,128]{3,2,1,0:T(8,128)S(1)}, f32[2,720,128]{2,1,0:T(8,...) custom-call(f32[8,64,128]{2,1,0:T(8,128)S(1)} %shard_map.69.own, ...), custom_call_target="tpu_custom_call" | custom-call | flops 2000000 | bytes 2000000 | tf_op jit(solution)/shard_map/pallas_call | solution.py:148
  20.0 1.3 %collective-permute-start.4 = (f32[8,128]{1,0:T(8,128)S(1)}, f32[8,128]{1,0:T(8,128)S(1)}, u32[]{:S(2)}, u32[]{:S(2)}) collective-permute-start(f32[8,128]{1,0:T(8,128)S(1)} %get-tuple-element.20.own), channel_id=1, source_target_pairs={{3,7},{7,11},{11,15},{15,19},{19,23},{23,27},{27,31},{31,35},{35,3... | collective-permute-start | bytes 12296 | tf_op jit(solution)/shard_map/ppermute | solution.py:503
  21.3 1.7 %shard_map.71 = (f32[2,720,128]{2,1,0:T(8,128)S(1)}, f32[8,128]{1,0:T(8,128)S(1)}) custom-call(f32[6,2,192,128]{3,2,1,0:T(8,128)S(1)} %get-tuple-element.21.co0, f32[6,2,96,128]{3,2,1,0:T(8,128)S(1)} %get-tuple-element.22.co1, f32[6,2,48,128]{3,2,1,0:T(8,128)S(1)} %get-tuple-element.23.co2, f32[6,2,24,128]{3,2,1,0:T(8,128)S(1)} %get-tuple-element.24.co3), custom_call_target="tpu_custom_call" | custom-call | flops 6000000 | bytes 6000000 | tf_op jit(solution)/shard_map/pallas_call | solution.py:148
  23.0 5.1 %collective-permute-done.4.crossed = f32[8,128]{1,0:T(8,128)S(1)} collective-permute-done((f32[8,128]{1,0:T(8,128)S(1)}, f32[8,128]{1,0:T(8,128)S(1)}, u32[]{:S(2)}, u32[]{:S(2)}) %collective-permute-start.4) | collective-permute-done | bytes 4128 | tf_op jit(solution)/shard_map/ppermute | solution.py:503
  28.1 16.4 %all_to_all.15 = f32[32,2,8,128]{3,2,1,0:T(8,128)S(1)} all-to-all(f32[32,2,8,128]{3,2,1,0:T(8,128)S(1)} %shard_map.72), channel_id=1, replica_groups=mesh['grp'=8,'z'=16,'x'=4] {'grp','x'}, dimensions={0} | all-to-all | bytes 524288 | tf_op jit(solution)/shard_map/all_to_all | solution.py:513
  44.5 3.4 %shard_map.73 = (f32[6,3,40,128]{3,2,1,0:T(8,128)S(1)}, f32[6,3,24,128]{3,2,1,0:T(8,128)S(1)}, f32[2,720,128]{2,1,0:T(8,128)S(1)}, f32[16,8,128]{2,1,0:T(8,128)S(1)}) custom-call(f32[64,8,128]{2,1,0:T(8,128)S(1)} %bitcast.1, f32[8,128]{1,0:T(8,128)S(1)} %get-tuple-element.25.responded, f32[6,2,192,128]{3,2,1,0:T(8,128)S(1)} %get-tuple-element.21.co0, ...), custom_call_target="tpu_custom_call" | custom-call | flops 2000000 | bytes 2000000 | tf_op jit(solution)/shard_map/pallas_call | solution.py:148
  47.9 27.5 %all_to_all.16.gathered = f32[16,8,128]{2,1,0:T(8,128)S(1)} all-to-all(f32[16,8,128]{2,1,0:T(8,128)S(1)} %get-tuple-element.27), channel_id=1, replica_groups=mesh['grp'=8,'z'=16,'x'=4] {'z'}, dimensions={0} | all-to-all | bytes 131072 | tf_op jit(solution)/shard_map/all_to_all | solution.py:533
  75.4 0.1 shard_map.74
  75.5 13.0 %all_to_all.17.gathered = f32[32,8,128]{2,1,0:T(8,128)S(1)} all-to-all(f32[32,8,128]{2,1,0:T(8,128)S(1)} %shard_map.74), channel_id=1, replica_groups=mesh['grp'=8,'z'=16,'x'=4] {'grp','x'}, dimensions={0} | all-to-all | bytes 262144 | tf_op jit(solution)/shard_map/all_to_all | solution.py:535
  88.5 2.6 %shard_map.75 = (f32[64,128]{1,0:T(8,128)}, f32[64,128]{1,0:T(8,128)}) custom-call(f32[32,8,128]{2,1,0:T(8,128)S(1)} %all_to_all.17.gathered, f32[6,2,192,128]{3,2,1,0:T(8,128)S(1)} %get-tuple-element.21.co0, f32[6,2,96,128]{3,2,1,0:T(8,128)S(1)} %get-tuple-element.22.co1, f32[6,2,48,128]{3,2,1,0:T(8,128)S(1)} %get-tuple-element.23.co2, ...), custom_call_target="tpu_custom_call" | custom-call | flops 2000000 | bytes 2000000 | tf_op jit(solution)/shard_map/pallas_call | solution.py:148
  (1 shorter events, 0.0 us)
Async XLA Ops:
  1.6 5.6 %collective-permute-start = (f32[2,64,128]{2,1,0:T(8,128)S(1)}, f32[2,64,128]{2,1,0:T(8,128)S(1)}, u32[]{:S(2)}, u32[]{:S(2)}) collective-permute-start(f32[2,64,128]{2,1,0:T(8,128)S(1)} %get-tuple-element.18), channel_id=1, source_target_pairs={{0,1},{2,3},{4,5},{6,7},{8,9},{10,11},{12,13},{14,15},{16,17},{18,... | collective-permute-start | bytes 196616 | tf_op jit(solution)/shard_map/ppermute | solution.py:475
  5.5 1.6 %collective-permute-start.1 = (f32[2,64,128]{2,1,0:T(8,128)S(1)}, f32[2,64,128]{2,1,0:T(8,128)S(1)}, u32[]{:S(2)}, u32[]{:S(2)}) collective-permute-start(f32[2,64,128]{2,1,0:T(8,128)S(1)} %get-tuple-element.19), channel_id=1, source_target_pairs={{1,2},{3,4},{5,6},{7,8},{9,10},{11,12},{13,14},{15,16},{17,18},{19... | collective-permute-start | bytes 196616 | tf_op jit(solution)/shard_map/ppermute | solution.py:476
  7.3 10.0 %collective-permute-start.3 = (f32[8,64,128]{2,1,0:T(8,128)S(1)}, f32[8,64,128]{2,1,0:T(8,128)S(1)}, u32[]{:S(2)}, u32[]{:S(2)}) collective-permute-start(f32[8,64,128]{2,1,0:T(8,128)S(1)} %shard_map.69.own), channel_id=1, source_target_pairs={{64,128},{192,256},{320,384},{128,64},{256,192},{384,320},{65,129}... | collective-permute-start | bytes 786440 | tf_op jit(solution)/shard_map/ppermute | solution.py:479
  12.5 6.0 %collective-permute-start.2 = (f32[8,64,128]{2,1,0:T(8,128)S(1)}, f32[8,64,128]{2,1,0:T(8,128)S(1)}, u32[]{:S(2)}, u32[]{:S(2)}) collective-permute-start(f32[8,64,128]{2,1,0:T(8,128)S(1)} %shard_map.69.own), channel_id=1, source_target_pairs={{0,64},{128,192},{256,320},{384,448},{64,0},{192,128},{320,256},{4... | collective-permute-start | bytes 786440 | tf_op jit(solution)/shard_map/ppermute | solution.py:478
  20.0 8.1 %collective-permute-start.4 = (f32[8,128]{1,0:T(8,128)S(1)}, f32[8,128]{1,0:T(8,128)S(1)}, u32[]{:S(2)}, u32[]{:S(2)}) collective-permute-start(f32[8,128]{1,0:T(8,128)S(1)} %get-tuple-element.20.own), channel_id=1, source_target_pairs={{3,7},{7,11},{11,15},{15,19},{19,23},{23,27},{27,31},{31,35},{35,3... | collective-permute-start | bytes 12296 | tf_op jit(solution)/shard_map/ppermute | solution.py:503

commit v4 on v3

--- a/solution.py
+++ b/solution.py
@@ -10,7 +10,7 @@
 RELAX = 0.8
 WET_MASS = 2e-05
 PAD = 8
-CHUNK = 32
+CHUNK = 16
 EAST, WEST, SOUTH, NORTH, MASS, RATE = range(6)
 
 
@@ -178,7 +178,7 @@
         second[k] = jnp.where(even, to_west, to_east)
 
 
-def widen(own, first, second, out):
+def widen(own, second, first, out):
     low = lanes((64, 128)) < 64
     even = lax.rem(lax.axis_index("x"), 2) == 0
     for k in range(2):
@@ -258,11 +258,15 @@
     packed[...] = out
 
 
-def fan(own, crossed, responded, out):
+def fan(own, first, second, responded, out):
+    even = lax.rem(lax.axis_index("x"), 2) == 0
+    east = jnp.where(even, first[...], second[...])
+    west = jnp.where(even, second[...], first[...])
     full = jnp.where((lanes((8, 128)) & 7) == 5, responded[...], own[...])
-    for k in range(out.shape[0]):
-        out[k, 0] = full
-        out[k, 1] = crossed[...]
+    for g in range(out.shape[0]):
+        out[g, 0] = west
+        out[g, 1] = full
+        out[g, 2] = east
 
 
 def ascend(coarse, bases, sources, to, temp, co):
@@ -335,14 +339,12 @@
     v0, v1, v2, b1, b2, b0 = state_of(before)
     v0a, v1a, v2a, b1a, b2a, _ = state_of(after)
     (t0, s0, t1, s1, t2, s2, r0, r1, r2, e3, bn, b3, b4, v3, s3, w3, v4, s4, r3, south_ref) = temps
-    group, own, inner_west, inner_east, at_west, at_east = neighbours()
-    at_west = 2 * at_west + jnp.where(inner_west, 0, 1)
-    at_east = 2 * at_east + jnp.where(inner_east, 0, 1)
+    group = lax.axis_index("grp")
     for t in range(5):
         at = group + (t - 2)
         valid = jnp.logical_and(at >= 0, at < 8).astype(F32)
-        at = 8 * jnp.clip(at, 0, 7)
-        x = jnp.concatenate([gathered[at + k] for k in (at_west, 2 * own, at_east)], axis=1) * valid
+        at = jnp.clip(at, 0, 7)
+        x = jnp.concatenate([gathered[at, k] for k in range(3)], axis=1) * valid
         row = 8 * t
         put(b3, row, spread(x, 0))
         put(co3, row, spread(x, 1), MASS)
@@ -474,7 +476,7 @@
     )
     first = lax.ppermute(first, dev, swaps(0, 64))
     second = lax.ppermute(second, dev, swaps(1, 64))
-    own = call(widen, field(8, 64, 128), [], own, first, second)
+    own = call(widen, field(8, 64, 128), [], own, second, first)
     first = lax.ppermute(own, "grp", swaps(0, 8))
     second = lax.ppermute(own, "grp", swaps(1, 8))
 
@@ -499,8 +501,8 @@
         first,
         second,
     )
-    crossings = [(4 * z + 3, 4 * z + 7) for z in range(15)] + [(4 * z + 4, 4 * z) for z in range(15)]
-    crossed = lax.ppermute(packed, dev, crossings)
+    first = lax.ppermute(packed, dev, swaps(0, 64))
+    second = lax.ppermute(packed, dev, swaps(1, 64))
     beside, responded = call(
         response,
         (state, field(8, 128)),
@@ -509,8 +511,8 @@
         near,
         cycles=3000,
     )
-    gathered = call(fan, field(32, 2, 8, 128), [], packed, crossed, responded)
-    gathered = lax.all_to_all(gathered, ("grp", "x"), 0, 0, tiled=True).reshape(64, 8, 128)
+    gathered = call(fan, field(8, 3, 8, 128), [], packed, first, second, responded)
+    gathered = lax.all_to_all(gathered, "grp", 0, 0, tiled=True)
     coarse = [shifted(40, 3), shifted(40, 3), shifted(40, 3), shifted(24, 3), shifted(24, 3)]
     *second, packed = call(
         second_leg,

time: 91.5 us -> 88.5 us (0.967)
  starting transfers between devices: 15.9 us -> 20.9 us
  waiting for transfers between devices: 7.2 us -> 3.03 us
  blocking collectives: 56.9 us -> 53.1 us
    all_to_all x1, blocking collectives: 16.4 us -> 10.4 us  [shards(): gathered = lax.all_to_all(gathered, 'grp', 0, 0, tiled=True)]
    ppermute x1 -> x2, waiting for transfers between devices: 5.1 us -> 0.02 us  [the longest x1 0.02 us: shards(): first = lax.ppermute(packed, dev, swaps(0, 64))]
    ppermute x1 -> x2, starting transfers between devices: 1.3 us -> 6.29 us  [the longest x1 5.62 us: shards(): first = lax.ppermute(packed, dev, swaps(0, 64))]
    ppermute x1, starting transfers between devices: 3.95 us -> 6.4 us  [shards(): first = lax.ppermute(first, dev, swaps(0, 64))]
    ppermute x1, starting transfers between devices: 4.87 us -> 2.66 us  [shards(): first = lax.ppermute(own, 'grp', swaps(0, 8))]
    all_to_all x1, blocking collectives: 27.5 us -> 29.5 us  [shards(): gathered = lax.all_to_all(packed, 'z', 0, 0, tiled=True)]
    ppermute x1, waiting for transfers between devices: 0.01 us -> 1.38 us  [shards(): second = lax.ppermute(own, 'grp', swaps(1, 8))]
    ppermute x1, waiting for transfers between devices: 1.13 us -> 0.01 us  [shards(): first = lax.ppermute(own, 'grp', swaps(0, 8))]
  transfers between devices with their start and end apart: 5 -> 6, of which waited for: 3 -> 2; matrix products, arithmetic and copies ran while one was open for 0% -> 0% of each run, Pallas kernels for 2% -> 2%
where the time goes in v4:
time: 88.5 us; the launch traced here: 88.1 us
  blocking collectives  53.1 us (60%)
  starting transfers between devices  20.9 us (24%)
  Pallas kernels  10.2 us (12%)
  waiting for transfers between devices  3.03 us (3%)
    all_to_all x1, blocking collectives, shards(): gathered = lax.all_to_all(packed, 'z', 0, 0, tiled=True)  29.5 us
    all_to_all x1, blocking collectives, shards(): gathered = lax.all_to_all(gathered, ('grp', 'x'), 0, 0, tiled=True)  13.2 us
    all_to_all x1, blocking collectives, shards(): gathered = lax.all_to_all(gathered, 'grp', 0, 0, tiled=True)  10.4 us
    pallas_call x8, Pallas kernels, call(): pl.pallas_call(body, out_shape=outs, in_specs=[pl.BlockSpec(memory_space=...  10.2 us
    ppermute x1, starting transfers between devices, shards(): first = lax.ppermute(first, dev, swaps(0, 64))  6.4 us
    ppermute x1, starting transfers between devices, shards(): first = lax.ppermute(packed, dev, swaps(0, 64))  5.62 us
    ppermute x1, starting transfers between devices, shards(): second = lax.ppermute(own, 'grp', swaps(1, 8))  4.91 us
    ppermute x1, starting transfers between devices, shards(): first = lax.ppermute(own, 'grp', swaps(0, 8))  2.66 us
  transfers between devices with their start and end apart: 6, of which 2 were waited for; matrix products, arithmetic and copies ran while one was open for 0% of the time, Pallas kernels for 2%

profile of v4, /device:TPU:1, one launch (start us, length us, event | category | flops | bytes accessed | tf_op | source)
XLA Modules:
  0.0 88.1 jit_solution(8742353290865291107)
XLA Ops:
  0.6 1.0 %shard_map.68 = (f32[4,64,128]{2,1,0:T(8,128)S(1)}, f32[2,64,128]{2,1,0:T(8,128)S(1)}, f32[2,64,128]{2,1,0:T(8,128)S(1)}) custom-call(f32[64,128]{1,0:T(8,128)} %refs_0_.1, f32[64,128]{1,0:T(8,128)} %refs_1_.1, f32[64,128]{1,0:T(8,128)} %refs_2_.1, f32[64,128]{1,0:T(8,128)} %refs_3_.1, s32[64,128]{1,0:T(8,128)} %refs_4_.1), custom_call_target="tpu_custom_call" | custom-call | flops 2000000 | bytes 2000000 | tf_op jit(solution)/shard_map/pallas_call | solution.py:148
  1.6 0.7 collective-permute-start
  2.3 6.4 %collective-permute-start.1 = (f32[2,64,128]{2,1,0:T(8,128)S(1)}, f32[2,64,128]{2,1,0:T(8,128)S(1)}, u32[]{:S(2)}, u32[]{:S(2)}) collective-permute-start(f32[2,64,128]{2,1,0:T(8,128)S(1)} %get-tuple-element.19), channel_id=1, source_target_pairs={{0,1},{2,3},{4,5},{6,7},{8,9},{10,11},{12,13},{14,15},{16,17},{18,... | collective-permute-start | bytes 196616 | tf_op jit(solution)/shard_map/ppermute | solution.py:477
  8.7 0.0 collective-permute-done.second
  8.7 1.6 %collective-permute-done.1.first = f32[2,64,128]{2,1,0:T(8,128)S(1)} collective-permute-done((f32[2,64,128]{2,1,0:T(8,128)S(1)}, f32[2,64,128]{2,1,0:T(8,128)S(1)}, u32[]{:S(2)}, u32[]{:S(2)}) %collective-permute-start.1) | collective-permute-done | bytes 65568 | tf_op jit(solution)/shard_map/ppermute | solution.py:477
  10.3 0.1 shard_map.69.own
  10.4 4.9 %collective-permute-start.3 = (f32[8,64,128]{2,1,0:T(8,128)S(1)}, f32[8,64,128]{2,1,0:T(8,128)S(1)}, u32[]{:S(2)}, u32[]{:S(2)}) collective-permute-start(f32[8,64,128]{2,1,0:T(8,128)S(1)} %shard_map.69.own), channel_id=1, source_target_pairs={{64,128},{192,256},{320,384},{128,64},{256,192},{384,320},{65,129}... | collective-permute-start | bytes 786440 | tf_op jit(solution)/shard_map/ppermute | solution.py:481
  15.3 2.7 %collective-permute-start.2 = (f32[8,64,128]{2,1,0:T(8,128)S(1)}, f32[8,64,128]{2,1,0:T(8,128)S(1)}, u32[]{:S(2)}, u32[]{:S(2)}) collective-permute-start(f32[8,64,128]{2,1,0:T(8,128)S(1)} %shard_map.69.own), channel_id=1, source_target_pairs={{0,64},{128,192},{256,320},{384,448},{64,0},{192,128},{320,256},{4... | collective-permute-start | bytes 786440 | tf_op jit(solution)/shard_map/ppermute | solution.py:480
  18.0 1.4 %collective-permute-done.3.second = f32[8,64,128]{2,1,0:T(8,128)S(1)} collective-permute-done((f32[8,64,128]{2,1,0:T(8,128)S(1)}, f32[8,64,128]{2,1,0:T(8,128)S(1)}, u32[]{:S(2)}, u32[]{:S(2)}) %collective-permute-start.3) | collective-permute-done | bytes 262176 | tf_op jit(solution)/shard_map/ppermute | solution.py:481
  19.4 0.0 collective-permute-done.2.first
  19.4 1.5 %shard_map.70 = (f32[6,2,192,128]{3,2,1,0:T(8,128)S(1)}, f32[6,2,96,128]{3,2,1,0:T(8,128)S(1)}, f32[6,2,48,128]{3,2,1,0:T(8,128)S(1)}, f32[2,720,128]{2,1,0:T(8,...) custom-call(f32[8,64,128]{2,1,0:T(8,128)S(1)} %shard_map.69.own, ...), custom_call_target="tpu_custom_call" | custom-call | flops 2000000 | bytes 2000000 | tf_op jit(solution)/shard_map/pallas_call | solution.py:148
  20.9 0.7 collective-permute-start.5
  21.6 5.6 %collective-permute-start.4 = (f32[8,128]{1,0:T(8,128)S(1)}, f32[8,128]{1,0:T(8,128)S(1)}, u32[]{:S(2)}, u32[]{:S(2)}) collective-permute-start(f32[8,128]{1,0:T(8,128)S(1)} %get-tuple-element.20.own), channel_id=1, source_target_pairs={{0,1},{2,3},{4,5},{6,7},{8,9},{10,11},{12,13},{14,15},{16,17},{18,... | collective-permute-start | bytes 12296 | tf_op jit(solution)/shard_map/ppermute | solution.py:504
  27.2 1.6 %shard_map.71 = (f32[2,720,128]{2,1,0:T(8,128)S(1)}, f32[8,128]{1,0:T(8,128)S(1)}) custom-call(f32[6,2,192,128]{3,2,1,0:T(8,128)S(1)} %get-tuple-element.21.co0, f32[6,2,96,128]{3,2,1,0:T(8,128)S(1)} %get-tuple-element.22.co1, f32[6,2,48,128]{3,2,1,0:T(8,128)S(1)} %get-tuple-element.23.co2, f32[6,2,24,128]{3,2,1,0:T(8,128)S(1)} %get-tuple-element.24.co3), custom_call_target="tpu_custom_call" | custom-call | flops 6000000 | bytes 6000000 | tf_op jit(solution)/shard_map/pallas_call | solution.py:148
  28.9 0.0 collective-permute-done.5.second
  28.9 0.0 collective-permute-done.4.first
  28.9 10.4 %all_to_all.15.gathered = f32[8,3,8,128]{3,2,1,0:T(8,128)S(1)} all-to-all(f32[8,3,8,128]{3,2,1,0:T(8,128)S(1)} %shard_map.72), channel_id=1, replica_groups=mesh['grp'=8,'z'=16,'x'=4] {'grp'}, dimensions={0} | all-to-all | bytes 196608 | tf_op jit(solution)/shard_map/all_to_all | solution.py:515
  39.3 3.3 %shard_map.73 = (f32[6,3,40,128]{3,2,1,0:T(8,128)S(1)}, f32[6,3,24,128]{3,2,1,0:T(8,128)S(1)}, f32[2,720,128]{2,1,0:T(8,128)S(1)}, f32[16,8,128]{2,1,0:T(8,128)S(1)}) custom-call(f32[8,3,8,128]{3,2,1,0:T(8,128)S(1)} %all_to_all.15.gathered, f32[8,128]{1,0:T(8,128)S(1)} %get-tuple-element.25.responded, f32[6,2,192,128]{3,2,1,0:T(8,128)S(1)} %get-tuple-element.21.co0, ...), custom_call_target="tpu_custom_call" | custom-call | flops 2000000 | bytes 2000000 | tf_op jit(solution)/shard_map/pallas_call | solution.py:148
  42.6 29.5 %all_to_all.16.gathered = f32[16,8,128]{2,1,0:T(8,128)S(1)} all-to-all(f32[16,8,128]{2,1,0:T(8,128)S(1)} %get-tuple-element.27), channel_id=1, replica_groups=mesh['grp'=8,'z'=16,'x'=4] {'z'}, dimensions={0} | all-to-all | bytes 131072 | tf_op jit(solution)/shard_map/all_to_all | solution.py:535
  72.1 0.1 shard_map.74
  72.2 13.2 %all_to_all.17.gathered = f32[32,8,128]{2,1,0:T(8,128)S(1)} all-to-all(f32[32,8,128]{2,1,0:T(8,128)S(1)} %shard_map.74), channel_id=1, replica_groups=mesh['grp'=8,'z'=16,'x'=4] {'grp','x'}, dimensions={0} | all-to-all | bytes 262144 | tf_op jit(solution)/shard_map/all_to_all | solution.py:537
  85.5 2.6 %shard_map.75 = (f32[64,128]{1,0:T(8,128)}, f32[64,128]{1,0:T(8,128)}) custom-call(f32[32,8,128]{2,1,0:T(8,128)S(1)} %all_to_all.17.gathered, f32[6,2,192,128]{3,2,1,0:T(8,128)S(1)} %get-tuple-element.21.co0, f32[6,2,96,128]{3,2,1,0:T(8,128)S(1)} %get-tuple-element.22.co1, f32[6,2,48,128]{3,2,1,0:T(8,128)S(1)} %get-tuple-element.23.co2, ...), custom_call_target="tpu_custom_call" | custom-call | flops 2000000 | bytes 2000000 | tf_op jit(solution)/shard_map/pallas_call | solution.py:148
  (1 shorter events, 0.0 us)
Async XLA Ops:
  1.6 7.1 %collective-permute-start = (f32[2,64,128]{2,1,0:T(8,128)S(1)}, f32[2,64,128]{2,1,0:T(8,128)S(1)}, u32[]{:S(2)}, u32[]{:S(2)}) collective-permute-start(f32[2,64,128]{2,1,0:T(8,128)S(1)} %get-tuple-element.18), channel_id=1, source_target_pairs={{1,2},{3,4},{5,6},{7,8},{9,10},{11,12},{13,14},{15,16},{17,18},{19... | collective-permute-start | bytes 196616 | tf_op jit(solution)/shard_map/ppermute | solution.py:478
  2.3 8.1 %collective-permute-start.1 = (f32[2,64,128]{2,1,0:T(8,128)S(1)}, f32[2,64,128]{2,1,0:T(8,128)S(1)}, u32[]{:S(2)}, u32[]{:S(2)}) collective-permute-start(f32[2,64,128]{2,1,0:T(8,128)S(1)} %get-tuple-element.19), channel_id=1, source_target_pairs={{0,1},{2,3},{4,5},{6,7},{8,9},{10,11},{12,13},{14,15},{16,17},{18,... | collective-permute-start | bytes 196616 | tf_op jit(solution)/shard_map/ppermute | solution.py:477
  10.4 9.0 %collective-permute-start.3 = (f32[8,64,128]{2,1,0:T(8,128)S(1)}, f32[8,64,128]{2,1,0:T(8,128)S(1)}, u32[]{:S(2)}, u32[]{:S(2)}) collective-permute-start(f32[8,64,128]{2,1,0:T(8,128)S(1)} %shard_map.69.own), channel_id=1, source_target_pairs={{64,128},{192,256},{320,384},{128,64},{256,192},{384,320},{65,129}... | collective-permute-start | bytes 786440 | tf_op jit(solution)/shard_map/ppermute | solution.py:481
  15.3 4.0 %collective-permute-start.2 = (f32[8,64,128]{2,1,0:T(8,128)S(1)}, f32[8,64,128]{2,1,0:T(8,128)S(1)}, u32[]{:S(2)}, u32[]{:S(2)}) collective-permute-start(f32[8,64,128]{2,1,0:T(8,128)S(1)} %shard_map.69.own), channel_id=1, source_target_pairs={{0,64},{128,192},{256,320},{384,448},{64,0},{192,128},{320,256},{4... | collective-permute-start | bytes 786440 | tf_op jit(solution)/shard_map/ppermute | solution.py:480
  20.9 8.0 %collective-permute-start.5 = (f32[8,128]{1,0:T(8,128)S(1)}, f32[8,128]{1,0:T(8,128)S(1)}, u32[]{:S(2)}, u32[]{:S(2)}) collective-permute-start(f32[8,128]{1,0:T(8,128)S(1)} %get-tuple-element.20.own), channel_id=1, source_target_pairs={{1,2},{3,4},{5,6},{7,8},{9,10},{11,12},{13,14},{15,16},{17,18},{19... | collective-permute-start | bytes 12296 | tf_op jit(solution)/shard_map/ppermute | solution.py:505
  21.6 7.3 %collective-permute-start.4 = (f32[8,128]{1,0:T(8,128)S(1)}, f32[8,128]{1,0:T(8,128)S(1)}, u32[]{:S(2)}, u32[]{:S(2)}) collective-permute-start(f32[8,128]{1,0:T(8,128)S(1)} %get-tuple-element.20.own), channel_id=1, source_target_pairs={{0,1},{2,3},{4,5},{6,7},{8,9},{10,11},{12,13},{14,15},{16,17},{18,... | collective-permute-start | bytes 12296 | tf_op jit(solution)/shard_map/ppermute | solution.py:504

commit v5 on v4

--- a/solution.py
+++ b/solution.py
@@ -262,11 +262,13 @@
     even = lax.rem(lax.axis_index("x"), 2) == 0
     east = jnp.where(even, first[...], second[...])
     west = jnp.where(even, second[...], first[...])
-    full = jnp.where((lanes((8, 128)) & 7) == 5, responded[...], own[...])
+    slot = lanes((8, 128)) & 7
+    one = jnp.where(slot < 5, own[...], pltpu.roll(west, 5, 1))
+    two = jnp.where(slot < 2, pltpu.roll(west, 125, 1), pltpu.roll(east, 2, 1))
+    two = jnp.where(slot == 7, responded[...], two)
     for g in range(out.shape[0]):
-        out[g, 0] = west
-        out[g, 1] = full
-        out[g, 2] = east
+        out[g, 0] = one
+        out[g, 1] = two
 
 
 def ascend(coarse, bases, sources, to, temp, co):
@@ -307,10 +309,8 @@
 
 
 def spread(x, slot):
-    y = jnp.where((lanes(x.shape) & 7) == slot, x, 0.0)
-    for step in (1, 2, 4):
-        y = pair_sum(y, step)
-    return y
+    at = jnp.bitwise_or(jnp.bitwise_and(lanes(x.shape), 120), slot)
+    return jnp.take_along_axis(x, at, axis=1, mode="promise_in_bounds")
 
 
 def inner_part(wide, to):
@@ -331,8 +331,8 @@
     if shift is not None:
         put(v4, PAD, get(v4, PAD, 24) + shift)
     prolong(v4, v3, v3, 0, 40)
-    sweep(v3, s3, co3, b3, 0, 40, 8)
-    sweep(s3, v3, co3, b3, 0, 40, 8)
+    sweep(v3, s3, co3, b3, 8, 32, 8)
+    sweep(s3, v3, co3, b3, 8, 32, 8)
 
 
 def second_leg(gathered, responded, co0, co1, co2, before, co3, co4, after, packed, *temps):
@@ -344,17 +344,22 @@
         at = group + (t - 2)
         valid = jnp.logical_and(at >= 0, at < 8).astype(F32)
         at = jnp.clip(at, 0, 7)
-        x = jnp.concatenate([gathered[at, k] for k in range(3)], axis=1) * valid
+        one, two = gathered[at, 0] * valid, gathered[at, 1] * valid
+
+        def wide(k):
+            west = spread(one, 5 + k) if k < 3 else spread(two, k - 3)
+            return jnp.concatenate([west, spread(one, k), spread(two, 2 + k)], axis=1)
+
         row = 8 * t
-        put(b3, row, spread(x, 0))
-        put(co3, row, spread(x, 1), MASS)
-        east = spread(x, 2)
+        put(b3, row, wide(0))
+        put(co3, row, wide(1), MASS)
+        east = wide(2)
         put(co3, row, east, EAST)
         put(co3, row, from_west(east, 8), WEST)
-        south = spread(x, 3)
+        south = wide(3)
         put(co3, row, south, SOUTH)
         put(south_ref, PAD + row, south)
-        d = spread(x, 4)
+        d = wide(4)
         put(co3, row, RELAX / jnp.where(d > 0, d, 1.0), RATE)
     for a, n in chunks(0, 40):
         put(co3, a, get(south_ref, PAD + a - 1, n), NORTH)
@@ -365,8 +370,8 @@
     for here, there in ((v4, s4), (s4, v4), (v4, s4), (s4, v4)):
         sweep(here, there, co4, None, 0, 24, 16)
     prolong(v4, None, w3, 0, 40)
-    sweep(w3, s3, co3, None, 0, 40, 8)
-    sweep(s3, w3, co3, None, 0, 40, 8)
+    sweep(w3, s3, co3, None, 8, 32, 8)
+    sweep(s3, w3, co3, None, 8, 32, 8)
     weight = w3[1, pl.ds(PAD + 16, 8), :]
 
     solve_coarse(b3, b4, co3, co4, v3, s3, v4, s4, r3, None)
@@ -426,8 +431,8 @@
         w, o, e = gathered[g + at_west], gathered[g + x], gathered[g + at_east]
         w = jnp.where(inner_west, w, pltpu.roll(w, 126, 1))
         e = jnp.where(inner_east, e, pltpu.roll(e, 124, 1))
-        both = jnp.concatenate([w, o, e], axis=1)
-        put(b3, 8 * t, spread(both + shift1 * from_east(both, 1), 0))
+        both = [spread(part + shift1 * from_east(part, 1), 0) for part in (w, o, e)]
+        put(b3, 8 * t, jnp.concatenate(both, axis=1))
     solve_coarse(b3, b4, co3, co4, v3, s3, v4, s4, r3, shift2)
     inner_part(v3, e3)
 
@@ -511,7 +516,7 @@
         near,
         cycles=3000,
     )
-    gathered = call(fan, field(8, 3, 8, 128), [], packed, first, second, responded)
+    gathered = call(fan, field(8, 2, 8, 128), [], packed, first, second, responded)
     gathered = lax.all_to_all(gathered, "grp", 0, 0, tiled=True)
     coarse = [shifted(40, 3), shifted(40, 3), shifted(40, 3), shifted(24, 3), shifted(24, 3)]
     *second, packed = call(

time: 88.5 us -> 87.9 us (level)
  no operation moved by 1% of the time
where the time goes in v5:
time: 87.9 us; the launch traced here: 87.5 us
  blocking collectives  53 us (60%)
  starting transfers between devices  20.9 us (24%)
  Pallas kernels  9.85 us (11%)
  waiting for transfers between devices  3.03 us (3%)
    all_to_all x1, blocking collectives, shards(): gathered = lax.all_to_all(packed, 'z', 0, 0, tiled=True)  29.5 us
    all_to_all x1, blocking collectives, shards(): gathered = lax.all_to_all(gathered, ('grp', 'x'), 0, 0, tiled=True)  13.2 us
    all_to_all x1, blocking collectives, shards(): gathered = lax.all_to_all(gathered, 'grp', 0, 0, tiled=True)  10.2 us
    pallas_call x8, Pallas kernels, call(): pl.pallas_call(body, out_shape=outs, in_specs=[pl.BlockSpec(memory_space=...  9.85 us
    ppermute x1, starting transfers between devices, shards(): first = lax.ppermute(first, dev, swaps(0, 64))  6.4 us
    ppermute x1, starting transfers between devices, shards(): first = lax.ppermute(packed, dev, swaps(0, 64))  5.62 us
    ppermute x1, starting transfers between devices, shards(): second = lax.ppermute(own, 'grp', swaps(1, 8))  4.91 us
    ppermute x1, starting transfers between devices, shards(): first = lax.ppermute(own, 'grp', swaps(0, 8))  2.66 us
  transfers between devices with their start and end apart: 6, of which 2 were waited for; matrix products, arithmetic and copies ran while one was open for 0% of the time, Pallas kernels for 2%

profile of v5, /device:TPU:1, one launch (start us, length us, event | category | flops | bytes accessed | tf_op | source)
XLA Modules:
  0.0 87.5 jit_solution(16714012061153041211)
XLA Ops:
  0.6 1.0 %shard_map.68 = (f32[4,64,128]{2,1,0:T(8,128)S(1)}, f32[2,64,128]{2,1,0:T(8,128)S(1)}, f32[2,64,128]{2,1,0:T(8,128)S(1)}) custom-call(f32[64,128]{1,0:T(8,128)} %refs_0_.1, f32[64,128]{1,0:T(8,128)} %refs_1_.1, f32[64,128]{1,0:T(8,128)} %refs_2_.1, f32[64,128]{1,0:T(8,128)} %refs_3_.1, s32[64,128]{1,0:T(8,128)} %refs_4_.1), custom_call_target="tpu_custom_call" | custom-call | flops 2000000 | bytes 2000000 | tf_op jit(solution)/shard_map/pallas_call | solution.py:148
  1.6 0.7 collective-permute-start
  2.3 6.4 %collective-permute-start.1 = (f32[2,64,128]{2,1,0:T(8,128)S(1)}, f32[2,64,128]{2,1,0:T(8,128)S(1)}, u32[]{:S(2)}, u32[]{:S(2)}) collective-permute-start(f32[2,64,128]{2,1,0:T(8,128)S(1)} %get-tuple-element.19), channel_id=1, source_target_pairs={{0,1},{2,3},{4,5},{6,7},{8,9},{10,11},{12,13},{14,15},{16,17},{18,... | collective-permute-start | bytes 196616 | tf_op jit(solution)/shard_map/ppermute | solution.py:482
  8.7 0.0 collective-permute-done.second
  8.7 1.6 %collective-permute-done.1.first = f32[2,64,128]{2,1,0:T(8,128)S(1)} collective-permute-done((f32[2,64,128]{2,1,0:T(8,128)S(1)}, f32[2,64,128]{2,1,0:T(8,128)S(1)}, u32[]{:S(2)}, u32[]{:S(2)}) %collective-permute-start.1) | collective-permute-done | bytes 65568 | tf_op jit(solution)/shard_map/ppermute | solution.py:482
  10.3 0.1 shard_map.69.own
  10.4 4.9 %collective-permute-start.3 = (f32[8,64,128]{2,1,0:T(8,128)S(1)}, f32[8,64,128]{2,1,0:T(8,128)S(1)}, u32[]{:S(2)}, u32[]{:S(2)}) collective-permute-start(f32[8,64,128]{2,1,0:T(8,128)S(1)} %shard_map.69.own), channel_id=1, source_target_pairs={{64,128},{192,256},{320,384},{128,64},{256,192},{384,320},{65,129}... | collective-permute-start | bytes 786440 | tf_op jit(solution)/shard_map/ppermute | solution.py:486
  15.3 2.7 %collective-permute-start.2 = (f32[8,64,128]{2,1,0:T(8,128)S(1)}, f32[8,64,128]{2,1,0:T(8,128)S(1)}, u32[]{:S(2)}, u32[]{:S(2)}) collective-permute-start(f32[8,64,128]{2,1,0:T(8,128)S(1)} %shard_map.69.own), channel_id=1, source_target_pairs={{0,64},{128,192},{256,320},{384,448},{64,0},{192,128},{320,256},{4... | collective-permute-start | bytes 786440 | tf_op jit(solution)/shard_map/ppermute | solution.py:485
  18.0 1.4 %collective-permute-done.3.second = f32[8,64,128]{2,1,0:T(8,128)S(1)} collective-permute-done((f32[8,64,128]{2,1,0:T(8,128)S(1)}, f32[8,64,128]{2,1,0:T(8,128)S(1)}, u32[]{:S(2)}, u32[]{:S(2)}) %collective-permute-start.3) | collective-permute-done | bytes 262176 | tf_op jit(solution)/shard_map/ppermute | solution.py:486
  19.4 0.0 collective-permute-done.2.first
  19.4 1.5 %shard_map.70 = (f32[6,2,192,128]{3,2,1,0:T(8,128)S(1)}, f32[6,2,96,128]{3,2,1,0:T(8,128)S(1)}, f32[6,2,48,128]{3,2,1,0:T(8,128)S(1)}, f32[2,720,128]{2,1,0:T(8,...) custom-call(f32[8,64,128]{2,1,0:T(8,128)S(1)} %shard_map.69.own, ...), custom_call_target="tpu_custom_call" | custom-call | flops 2000000 | bytes 2000000 | tf_op jit(solution)/shard_map/pallas_call | solution.py:148
  20.9 0.7 collective-permute-start.5
  21.6 5.6 %collective-permute-start.4 = (f32[8,128]{1,0:T(8,128)S(1)}, f32[8,128]{1,0:T(8,128)S(1)}, u32[]{:S(2)}, u32[]{:S(2)}) collective-permute-start(f32[8,128]{1,0:T(8,128)S(1)} %get-tuple-element.20.own), channel_id=1, source_target_pairs={{0,1},{2,3},{4,5},{6,7},{8,9},{10,11},{12,13},{14,15},{16,17},{18,... | collective-permute-start | bytes 12296 | tf_op jit(solution)/shard_map/ppermute | solution.py:509
  27.2 1.6 %shard_map.71 = (f32[2,720,128]{2,1,0:T(8,128)S(1)}, f32[8,128]{1,0:T(8,128)S(1)}) custom-call(f32[6,2,192,128]{3,2,1,0:T(8,128)S(1)} %get-tuple-element.21.co0, f32[6,2,96,128]{3,2,1,0:T(8,128)S(1)} %get-tuple-element.22.co1, f32[6,2,48,128]{3,2,1,0:T(8,128)S(1)} %get-tuple-element.23.co2, f32[6,2,24,128]{3,2,1,0:T(8,128)S(1)} %get-tuple-element.24.co3), custom_call_target="tpu_custom_call" | custom-call | flops 6000000 | bytes 6000000 | tf_op jit(solution)/shard_map/pallas_call | solution.py:148
  28.9 0.0 collective-permute-done.5.second
  28.9 0.0 collective-permute-done.4.first
  28.9 0.1 shard_map.72
  29.0 10.2 %all_to_all.15.gathered = f32[8,2,8,128]{3,2,1,0:T(8,128)S(1)} all-to-all(f32[8,2,8,128]{3,2,1,0:T(8,128)S(1)} %shard_map.72), channel_id=1, replica_groups=mesh['grp'=8,'z'=16,'x'=4] {'grp'}, dimensions={0} | all-to-all | bytes 131072 | tf_op jit(solution)/shard_map/all_to_all | solution.py:520
  39.2 3.1 %shard_map.73 = (f32[6,3,40,128]{3,2,1,0:T(8,128)S(1)}, f32[6,3,24,128]{3,2,1,0:T(8,128)S(1)}, f32[2,720,128]{2,1,0:T(8,128)S(1)}, f32[16,8,128]{2,1,0:T(8,128)S(1)}) custom-call(f32[8,2,8,128]{3,2,1,0:T(8,128)S(1)} %all_to_all.15.gathered, f32[8,128]{1,0:T(8,128)S(1)} %get-tuple-element.25.responded, f32[6,2,192,128]{3,2,1,0:T(8,128)S(1)} %get-tuple-element.21.co0, ...), custom_call_target="tpu_custom_call" | custom-call | flops 2000000 | bytes 2000000 | tf_op jit(solution)/shard_map/pallas_call | solution.py:148
  42.3 29.5 %all_to_all.16.gathered = f32[16,8,128]{2,1,0:T(8,128)S(1)} all-to-all(f32[16,8,128]{2,1,0:T(8,128)S(1)} %get-tuple-element.27), channel_id=1, replica_groups=mesh['grp'=8,'z'=16,'x'=4] {'z'}, dimensions={0} | all-to-all | bytes 131072 | tf_op jit(solution)/shard_map/all_to_all | solution.py:540
  71.8 0.1 shard_map.74
  71.9 13.2 %all_to_all.17.gathered = f32[32,8,128]{2,1,0:T(8,128)S(1)} all-to-all(f32[32,8,128]{2,1,0:T(8,128)S(1)} %shard_map.74), channel_id=1, replica_groups=mesh['grp'=8,'z'=16,'x'=4] {'grp','x'}, dimensions={0} | all-to-all | bytes 262144 | tf_op jit(solution)/shard_map/all_to_all | solution.py:542
  85.1 2.4 %shard_map.75 = (f32[64,128]{1,0:T(8,128)}, f32[64,128]{1,0:T(8,128)}) custom-call(f32[32,8,128]{2,1,0:T(8,128)S(1)} %all_to_all.17.gathered, f32[6,2,192,128]{3,2,1,0:T(8,128)S(1)} %get-tuple-element.21.co0, f32[6,2,96,128]{3,2,1,0:T(8,128)S(1)} %get-tuple-element.22.co1, f32[6,2,48,128]{3,2,1,0:T(8,128)S(1)} %get-tuple-element.23.co2, ...), custom_call_target="tpu_custom_call" | custom-call | flops 2000000 | bytes 2000000 | tf_op jit(solution)/shard_map/pallas_call | solution.py:148
Async XLA Ops:
  1.6 7.1 %collective-permute-start = (f32[2,64,128]{2,1,0:T(8,128)S(1)}, f32[2,64,128]{2,1,0:T(8,128)S(1)}, u32[]{:S(2)}, u32[]{:S(2)}) collective-permute-start(f32[2,64,128]{2,1,0:T(8,128)S(1)} %get-tuple-element.18), channel_id=1, source_target_pairs={{1,2},{3,4},{5,6},{7,8},{9,10},{11,12},{13,14},{15,16},{17,18},{19... | collective-permute-start | bytes 196616 | tf_op jit(solution)/shard_map/ppermute | solution.py:483
  2.3 8.1 %collective-permute-start.1 = (f32[2,64,128]{2,1,0:T(8,128)S(1)}, f32[2,64,128]{2,1,0:T(8,128)S(1)}, u32[]{:S(2)}, u32[]{:S(2)}) collective-permute-start(f32[2,64,128]{2,1,0:T(8,128)S(1)} %get-tuple-element.19), channel_id=1, source_target_pairs={{0,1},{2,3},{4,5},{6,7},{8,9},{10,11},{12,13},{14,15},{16,17},{18,... | collective-permute-start | bytes 196616 | tf_op jit(solution)/shard_map/ppermute | solution.py:482
  10.4 9.0 %collective-permute-start.3 = (f32[8,64,128]{2,1,0:T(8,128)S(1)}, f32[8,64,128]{2,1,0:T(8,128)S(1)}, u32[]{:S(2)}, u32[]{:S(2)}) collective-permute-start(f32[8,64,128]{2,1,0:T(8,128)S(1)} %shard_map.69.own), channel_id=1, source_target_pairs={{64,128},{192,256},{320,384},{128,64},{256,192},{384,320},{65,129}... | collective-permute-start | bytes 786440 | tf_op jit(solution)/shard_map/ppermute | solution.py:486
  15.3 4.0 %collective-permute-start.2 = (f32[8,64,128]{2,1,0:T(8,128)S(1)}, f32[8,64,128]{2,1,0:T(8,128)S(1)}, u32[]{:S(2)}, u32[]{:S(2)}) collective-permute-start(f32[8,64,128]{2,1,0:T(8,128)S(1)} %shard_map.69.own), channel_id=1, source_target_pairs={{0,64},{128,192},{256,320},{384,448},{64,0},{192,128},{320,256},{4... | collective-permute-start | bytes 786440 | tf_op jit(solution)/shard_map/ppermute | solution.py:485
  20.9 8.0 %collective-permute-start.5 = (f32[8,128]{1,0:T(8,128)S(1)}, f32[8,128]{1,0:T(8,128)S(1)}, u32[]{:S(2)}, u32[]{:S(2)}) collective-permute-start(f32[8,128]{1,0:T(8,128)S(1)} %get-tuple-element.20.own), channel_id=1, source_target_pairs={{1,2},{3,4},{5,6},{7,8},{9,10},{11,12},{13,14},{15,16},{17,18},{19... | collective-permute-start | bytes 12296 | tf_op jit(solution)/shard_map/ppermute | solution.py:510
  21.6 7.3 %collective-permute-start.4 = (f32[8,128]{1,0:T(8,128)S(1)}, f32[8,128]{1,0:T(8,128)S(1)}, u32[]{:S(2)}, u32[]{:S(2)}) collective-permute-start(f32[8,128]{1,0:T(8,128)S(1)} %get-tuple-element.20.own), channel_id=1, source_target_pairs={{0,1},{2,3},{4,5},{6,7},{8,9},{10,11},{12,13},{14,15},{16,17},{18,... | collective-permute-start | bytes 12296 | tf_op jit(solution)/shard_map/ppermute | solution.py:509

commit v6 on v5

--- a/solution.py
+++ b/solution.py
@@ -178,16 +178,41 @@
         second[k] = jnp.where(even, to_west, to_east)
 
 
-def widen(own, second, first, out):
+def widen(own, second, first, out, near, far, wet_ref, before_ref, south_ref):
     low = lanes((64, 128)) < 64
     even = lax.rem(lax.axis_index("x"), 2) == 0
     for k in range(2):
         e = jnp.where(even, first[k], second[k])
         w = jnp.where(even, second[k], first[k])
-        out[2 * k] = own[2 * k]
-        out[2 * k + 1] = own[2 * k + 1]
-        out[4 + 2 * k] = jnp.where(low, e, w)
-        out[5 + 2 * k] = jnp.where(low, pltpu.roll(e, 64, 1), pltpu.roll(w, 64, 1))
+        for p, (east, west) in enumerate(((e, w), (pltpu.roll(e, 64, 1), pltpu.roll(w, 64, 1)))):
+            out[0, pl.ds(64 * (2 * k + p), 64), :] = own[2 * k + p]
+            out[1, pl.ds(64 * (2 * k + p), 64), :] = jnp.where(low, east, west)
+    for ref in (wet_ref, before_ref, south_ref):
+        for edge in (0, PAD + 64):
+            put(ref, edge, jnp.zeros((PAD, 256), F32))
+    for a, n in chunks(0, 64):
+        put(wet_ref, PAD + a, jnp.where(get(out, a, n) > 0, 1.0, 0.0))
+        put(before_ref, PAD + a, get(out, 192 + a, n))
+    for a, n in chunks(0, 64):
+        put(south_ref, PAD + a, get(out, 64 + a, n) * get(wet_ref, PAD + a + 1, n))
+    for a, n in chunks(0, 64):
+        wet, v = get(wet_ref, PAD + a, n), get(before_ref, PAD + a, n)
+        east = get(out, a, n) * from_east(wet, 1)
+        applied = (
+            (wet * WET_MASS + (1.0 - wet)) * v
+            + east * (v - from_east(v, 1))
+            + from_west(east, 1) * (v - from_west(v, 1))
+            + get(south_ref, PAD + a, n) * (v - get(before_ref, PAD + a + 1, n))
+            + get(south_ref, PAD + a - 1, n) * (v - get(before_ref, PAD + a - 1, n))
+        )
+        put(out, 128 + a, get(out, 128 + a, n) - applied)
+    group_even = lax.rem(lax.axis_index("grp"), 2) == 0
+    for k in range(4):
+        count = 56 if k < 3 else 8
+        for h in range(2):
+            up, down = out[h, pl.ds(64 * k, count), :], out[h, pl.ds(64 * k + 64 - count, count), :]
+            near[h, pl.ds(56 * k, count), :] = jnp.where(group_even, down, up)
+            far[h, pl.ds(56 * k, count), :] = jnp.where(group_even, up, down)
 
 
 def descend(v1_ref, v2_ref, b1_ref, b2_ref, b3_ref, co, rest, temp, ranges):
@@ -203,24 +228,28 @@
     restrict(rest[2], b3_ref, l3, h3, 4)
 
 
-def first_leg(own, first, second, co0, co1, co2, state, co3, packed, *temps):
+def first_leg(own, far, near, co0, co1, co2, state, co3, packed, *temps):
     v0, v1, v2, b1, b2, b0 = state_of(state)
     wet_ref, south_ref, t0, t1, t2, r0, r1, r2, b3 = temps
     even = lax.rem(lax.axis_index("grp"), 2) == 0
 
+    def above(start, n):
+        return jnp.where(even, get(far, start, n), get(near, start, n))
+
+    def below(start, n):
+        return jnp.where(even, get(near, start, n), get(far, start, n))
+
     def window(k, a, n):
-        part, o = a // 64, a % 64
-        if part == 1:
-            return jnp.concatenate([own[k, o : o + n, :], own[4 + k, o : o + n, :]], axis=1)
-        up, down = (second, first) if part == 0 else (first, second)
-        halves = [jnp.where(even, up[h, o : o + n, :], down[h, o : o + n, :]) for h in (k, 4 + k)]
-        return jnp.concatenate(halves, axis=1)
-
-    for a, n in chunks(0, 192):
+        if a < 8 or a >= 184:
+            return jnp.zeros((n, 256), F32)
+        if a < 64:
+            return above(56 * k + a - 8, n)
+        return get(own, 64 * k + a - 64, n) if a < 128 else below(56 * k + a - 128, n)
+
+    for a, n in chunks(0, 192, 8):
         put(wet_ref, PAD + a, jnp.where(window(0, a, n) > 0, 1.0, 0.0))
-        put(v0, PAD + a, window(3, a, n))
         put(b0, a, window(2, a, n))
-    for a, n in chunks(0, 192):
+    for a, n in chunks(0, 192, 8):
         wet = get(wet_ref, PAD + a, n)
         east = window(0, a, n) * from_east(wet, 1)
         south = window(1, a, n) * get(wet_ref, PAD + a + 1, n)
@@ -229,6 +258,11 @@
         put(co0, a, south, SOUTH)
         put(south_ref, PAD + a, south)
         put(co0, a, wet * WET_MASS + (1.0 - wet), MASS)
+    edges = ((63, above(175, 1), get(own, 192, 1)), (127, get(own, 255, 1), below(168, 1)))
+    for row, here, next_row in edges:
+        flow = get(co0, row, 1, SOUTH) * (here - next_row)
+        put(b0, row, get(b0, row, 1) - flow)
+        put(b0, row + 1, get(b0, row + 1, 1) + flow)
     for a, n in chunks(0, 192):
         put(co0, a, get(south_ref, PAD + a - 1, n), NORTH)
     set_rate(co0, 192)
@@ -238,7 +272,7 @@
     set_rate(co2, 48)
     coarsen(co2, co3, 24, 4)
     set_rate(co3, 24)
-    sweep(v0, t0, co0, b0, 0, 192, 1)
+    first_sweep(t0, co0, b0, 0, 192)
     sweep(t0, v0, co0, b0, 0, 192, 1)
     residual(v0, r0, co0, b0, 0, 192, 1)
     descend(
@@ -409,7 +443,7 @@
         out[k] = value
 
 
-def third_leg(gathered, co0, co1, co2, before, co3, co4, after, beside, *others):
+def third_leg(gathered, own, co0, co1, co2, before, co3, co4, after, beside, *others):
     b0 = state_of(before)[5]
     v0a, v1a, v2a, b1a, b2a, _ = state_of(after)
     v0b, v1b, v2b, b1b, b2b, _ = state_of(beside)
@@ -454,7 +488,7 @@
     prolong(t1, c0, t0, 56, 136)
     sweep(t0, s0, co0, b0, 56, 136, 1)
     sweep(s0, t0, co0, b0, 56, 136, 1)
-    surface[...] = t0[0, pl.ds(PAD + 64, 64), :]
+    surface[...] = own[0, pl.ds(192, 64), :] + t0[0, pl.ds(PAD + 64, 64), :]
     for a, n in chunks(64, 128):
         _, out = operate(t0, co0, a, n, 1)
         rest[a - 64 : a - 64 + n, :] = b0[0, a : a + n, :] - out[:, :128]
@@ -481,9 +515,16 @@
     )
     first = lax.ppermute(first, dev, swaps(0, 64))
     second = lax.ppermute(second, dev, swaps(1, 64))
-    own = call(widen, field(8, 64, 128), [], own, second, first)
-    first = lax.ppermute(own, "grp", swaps(0, 8))
-    second = lax.ppermute(own, "grp", swaps(1, 8))
+    own, near, far = call(
+        widen,
+        (field(2, 256, 128), field(2, 176, 128), field(2, 176, 128)),
+        [scratch(2, 80, 128)] * 3,
+        own,
+        second,
+        first,
+    )
+    far = lax.ppermute(far, "grp", swaps(1, 8))
+    near = lax.ppermute(near, "grp", swaps(0, 8))
 
     def rows(count, planes=2):
         return field(planes, count, 128)
@@ -503,8 +544,8 @@
         (*co[:3], state, co[3], field(8, 128)),
         as_scratch(fine[0], fine[0], *fine, *sources, rows(24)),
         own,
-        first,
-        second,
+        far,
+        near,
     )
     first = lax.ppermute(packed, dev, swaps(0, 64))
     second = lax.ppermute(packed, dev, swaps(1, 64))
@@ -559,6 +600,7 @@
             rows(48, 3),
         ),
         gathered,
+        own,
         *kept,
         *second,
         beside,

time: 87.9 us -> 87.1 us (level)
  transfers between devices with their start and end apart: 6 -> 6, of which waited for: 2 -> 3; matrix products, arithmetic and copies ran while one was open for 0% -> 0% of each run, Pallas kernels for 2% -> 2%
where the time goes in v6:
time: 87.1 us; the launch traced here: 86.6 us
  blocking collectives  52.8 us (61%)
  starting transfers between devices  20.6 us (24%)
  Pallas kernels  9.87 us (11%)
  waiting for transfers between devices  2.68 us (3%)
    all_to_all x1, blocking collectives, shards(): gathered = lax.all_to_all(packed, 'z', 0, 0, tiled=True)  29.5 us
    all_to_all x1, blocking collectives, shards(): gathered = lax.all_to_all(gathered, ('grp', 'x'), 0, 0, tiled=True)  13.2 us
    all_to_all x1, blocking collectives, shards(): gathered = lax.all_to_all(gathered, 'grp', 0, 0, tiled=True)  10.1 us
    pallas_call x8, Pallas kernels, call(): pl.pallas_call(body, out_shape=outs, in_specs=[pl.BlockSpec(memory_space=...  9.87 us
    ppermute x1, starting transfers between devices, shards(): first = lax.ppermute(first, dev, swaps(0, 64))  6.4 us
    ppermute x1, starting transfers between devices, shards(): first = lax.ppermute(packed, dev, swaps(0, 64))  5.25 us
    ppermute x1, starting transfers between devices, shards(): far = lax.ppermute(far, 'grp', swaps(1, 8))  4.91 us
    ppermute x1, starting transfers between devices, shards(): near = lax.ppermute(near, 'grp', swaps(0, 8))  2.65 us
  transfers between devices with their start and end apart: 6, of which 3 were waited for; matrix products, arithmetic and copies ran while one was open for 0% of the time, Pallas kernels for 2%

profile of v6, /device:TPU:1, one launch (start us, length us, event | category | flops | bytes accessed | tf_op | source)
XLA Modules:
  0.0 86.6 jit_solution(279744004617784987)
XLA Ops:
  0.6 1.0 %shard_map.68 = (f32[4,64,128]{2,1,0:T(8,128)S(1)}, f32[2,64,128]{2,1,0:T(8,128)S(1)}, f32[2,64,128]{2,1,0:T(8,128)S(1)}) custom-call(f32[64,128]{1,0:T(8,128)} %refs_0_.1, f32[64,128]{1,0:T(8,128)} %refs_1_.1, f32[64,128]{1,0:T(8,128)} %refs_2_.1, f32[64,128]{1,0:T(8,128)} %refs_3_.1, s32[64,128]{1,0:T(8,128)} %refs_4_.1), custom_call_target="tpu_custom_call" | custom-call | flops 2000000 | bytes 2000000 | tf_op jit(solution)/shard_map/pallas_call | solution.py:148
  1.6 0.7 collective-permute-start
  2.3 6.4 %collective-permute-start.1 = (f32[2,64,128]{2,1,0:T(8,128)S(1)}, f32[2,64,128]{2,1,0:T(8,128)S(1)}, u32[]{:S(2)}, u32[]{:S(2)}) collective-permute-start(f32[2,64,128]{2,1,0:T(8,128)S(1)} %get-tuple-element.22), channel_id=1, source_target_pairs={{0,1},{2,3},{4,5},{6,7},{8,9},{10,11},{12,13},{14,15},{16,17},{18,... | collective-permute-start | bytes 196616 | tf_op jit(solution)/shard_map/ppermute | solution.py:516
  8.7 0.0 collective-permute-done.second
  8.7 1.6 %collective-permute-done.1.first = f32[2,64,128]{2,1,0:T(8,128)S(1)} collective-permute-done((f32[2,64,128]{2,1,0:T(8,128)S(1)}, f32[2,64,128]{2,1,0:T(8,128)S(1)}, u32[]{:S(2)}, u32[]{:S(2)}) %collective-permute-start.1) | collective-permute-done | bytes 65568 | tf_op jit(solution)/shard_map/ppermute | solution.py:516
  10.3 0.2 shard_map.69
  10.5 4.9 %collective-permute-start.2 = (f32[2,176,128]{2,1,0:T(8,128)S(1)}, f32[2,176,128]{2,1,0:T(8,128)S(1)}, u32[]{:S(2)}, u32[]{:S(2)}) collective-permute-start(f32[2,176,128]{2,1,0:T(8,128)S(1)} %get-tuple-element.24), channel_id=1, source_target_pairs={{64,128},{192,256},{320,384},{128,64},{256,192},{384,320},{65,129}... | collective-permute-start | bytes 540680 | tf_op jit(solution)/shard_map/ppermute | solution.py:526
  15.5 2.7 %collective-permute-start.3 = (f32[2,176,128]{2,1,0:T(8,128)S(1)}, f32[2,176,128]{2,1,0:T(8,128)S(1)}, u32[]{:S(2)}, u32[]{:S(2)}) collective-permute-start(f32[2,176,128]{2,1,0:T(8,128)S(1)} %get-tuple-element.25), channel_id=1, source_target_pairs={{0,64},{128,192},{256,320},{384,448},{64,0},{192,128},{320,256},{4... | collective-permute-start | bytes 540680 | tf_op jit(solution)/shard_map/ppermute | solution.py:527
  18.1 0.5 collective-permute-done.2.far
  18.6 0.5 collective-permute-done.3.near
  19.1 1.4 %shard_map.70 = (f32[6,2,192,128]{3,2,1,0:T(8,128)S(1)}, f32[6,2,96,128]{3,2,1,0:T(8,128)S(1)}, f32[6,2,48,128]{3,2,1,0:T(8,128)S(1)}, f32[2,720,128]{2,1,0:T(8,...) custom-call(f32[2,256,128]{2,1,0:T(8,128)S(1)} %get-tuple-element.23.own, ...), custom_call_target="tpu_custom_call" | custom-call | flops 2000000 | bytes 2000000 | tf_op jit(solution)/shard_map/pallas_call | solution.py:148
  20.6 0.7 collective-permute-start.5
  21.2 5.2 %collective-permute-start.4 = (f32[8,128]{1,0:T(8,128)S(1)}, f32[8,128]{1,0:T(8,128)S(1)}, u32[]{:S(2)}, u32[]{:S(2)}) collective-permute-start(f32[8,128]{1,0:T(8,128)S(1)} %get-tuple-element.26.own), channel_id=1, source_target_pairs={{0,1},{2,3},{4,5},{6,7},{8,9},{10,11},{12,13},{14,15},{16,17},{18,... | collective-permute-start | bytes 12296 | tf_op jit(solution)/shard_map/ppermute | solution.py:550
  26.5 1.6 %shard_map.71 = (f32[2,720,128]{2,1,0:T(8,128)S(1)}, f32[8,128]{1,0:T(8,128)S(1)}) custom-call(f32[6,2,192,128]{3,2,1,0:T(8,128)S(1)} %get-tuple-element.27.co0, f32[6,2,96,128]{3,2,1,0:T(8,128)S(1)} %get-tuple-element.28.co1, f32[6,2,48,128]{3,2,1,0:T(8,128)S(1)} %get-tuple-element.29.co2, f32[6,2,24,128]{3,2,1,0:T(8,128)S(1)} %get-tuple-element.30.co3), custom_call_target="tpu_custom_call" | custom-call | flops 6000000 | bytes 6000000 | tf_op jit(solution)/shard_map/pallas_call | solution.py:148
  28.1 0.0 collective-permute-done.5.second
  28.1 0.0 collective-permute-done.4.first
  28.2 0.1 shard_map.72
  28.3 10.1 %all_to_all.15.gathered = f32[8,2,8,128]{3,2,1,0:T(8,128)S(1)} all-to-all(f32[8,2,8,128]{3,2,1,0:T(8,128)S(1)} %shard_map.72), channel_id=1, replica_groups=mesh['grp'=8,'z'=16,'x'=4] {'grp'}, dimensions={0} | all-to-all | bytes 131072 | tf_op jit(solution)/shard_map/all_to_all | solution.py:561
  38.3 3.1 %shard_map.73 = (f32[6,3,40,128]{3,2,1,0:T(8,128)S(1)}, f32[6,3,24,128]{3,2,1,0:T(8,128)S(1)}, f32[2,720,128]{2,1,0:T(8,128)S(1)}, f32[16,8,128]{2,1,0:T(8,128)S(1)}) custom-call(f32[8,2,8,128]{3,2,1,0:T(8,128)S(1)} %all_to_all.15.gathered, f32[8,128]{1,0:T(8,128)S(1)} %get-tuple-element.31.responded, f32[6,2,192,128]{3,2,1,0:T(8,128)S(1)} %get-tuple-element.27.co0, ...), custom_call_target="tpu_custom_call" | custom-call | flops 2000000 | bytes 2000000 | tf_op jit(solution)/shard_map/pallas_call | solution.py:148
  41.4 29.5 %all_to_all.16.gathered = f32[16,8,128]{2,1,0:T(8,128)S(1)} all-to-all(f32[16,8,128]{2,1,0:T(8,128)S(1)} %get-tuple-element.33), channel_id=1, replica_groups=mesh['grp'=8,'z'=16,'x'=4] {'z'}, dimensions={0} | all-to-all | bytes 131072 | tf_op jit(solution)/shard_map/all_to_all | solution.py:581
  71.0 0.1 shard_map.74
  71.0 13.2 %all_to_all.17.gathered = f32[32,8,128]{2,1,0:T(8,128)S(1)} all-to-all(f32[32,8,128]{2,1,0:T(8,128)S(1)} %shard_map.74), channel_id=1, replica_groups=mesh['grp'=8,'z'=16,'x'=4] {'grp','x'}, dimensions={0} | all-to-all | bytes 262144 | tf_op jit(solution)/shard_map/all_to_all | solution.py:583
  84.3 2.4 %shard_map.75 = (f32[64,128]{1,0:T(8,128)}, f32[64,128]{1,0:T(8,128)}) custom-call(f32[32,8,128]{2,1,0:T(8,128)S(1)} %all_to_all.17.gathered, f32[2,256,128]{2,1,0:T(8,128)S(1)} %get-tuple-element.23.own, f32[6,2,192,128]{3,2,1,0:T(8,128)S(1)} %get-tuple-element.27.co0, f32[6,2,96,128]{3,2,1,0:T(8,128)S(1)} %get-tuple-element.28.co1, ...), custom_call_target="tpu_custom_call" | custom-call | flops 2000000 | bytes 2000000 | tf_op jit(solution)/shard_map/pallas_call | solution.py:148
Async XLA Ops:
  1.6 7.1 %collective-permute-start = (f32[2,64,128]{2,1,0:T(8,128)S(1)}, f32[2,64,128]{2,1,0:T(8,128)S(1)}, u32[]{:S(2)}, u32[]{:S(2)}) collective-permute-start(f32[2,64,128]{2,1,0:T(8,128)S(1)} %get-tuple-element.21), channel_id=1, source_target_pairs={{1,2},{3,4},{5,6},{7,8},{9,10},{11,12},{13,14},{15,16},{17,18},{19... | collective-permute-start | bytes 196616 | tf_op jit(solution)/shard_map/ppermute | solution.py:517
  2.3 8.1 %collective-permute-start.1 = (f32[2,64,128]{2,1,0:T(8,128)S(1)}, f32[2,64,128]{2,1,0:T(8,128)S(1)}, u32[]{:S(2)}, u32[]{:S(2)}) collective-permute-start(f32[2,64,128]{2,1,0:T(8,128)S(1)} %get-tuple-element.22), channel_id=1, source_target_pairs={{0,1},{2,3},{4,5},{6,7},{8,9},{10,11},{12,13},{14,15},{16,17},{18,... | collective-permute-start | bytes 196616 | tf_op jit(solution)/shard_map/ppermute | solution.py:516
  10.5 8.1 %collective-permute-start.2 = (f32[2,176,128]{2,1,0:T(8,128)S(1)}, f32[2,176,128]{2,1,0:T(8,128)S(1)}, u32[]{:S(2)}, u32[]{:S(2)}) collective-permute-start(f32[2,176,128]{2,1,0:T(8,128)S(1)} %get-tuple-element.24), channel_id=1, source_target_pairs={{64,128},{192,256},{320,384},{128,64},{256,192},{384,320},{65,129}... | collective-permute-start | bytes 540680 | tf_op jit(solution)/shard_map/ppermute | solution.py:526
  15.5 3.7 %collective-permute-start.3 = (f32[2,176,128]{2,1,0:T(8,128)S(1)}, f32[2,176,128]{2,1,0:T(8,128)S(1)}, u32[]{:S(2)}, u32[]{:S(2)}) collective-permute-start(f32[2,176,128]{2,1,0:T(8,128)S(1)} %get-tuple-element.25), channel_id=1, source_target_pairs={{0,64},{128,192},{256,320},{384,448},{64,0},{192,128},{320,256},{4... | collective-permute-start | bytes 540680 | tf_op jit(solution)/shard_map/ppermute | solution.py:527
  20.6 7.6 %collective-permute-start.5 = (f32[8,128]{1,0:T(8,128)S(1)}, f32[8,128]{1,0:T(8,128)S(1)}, u32[]{:S(2)}, u32[]{:S(2)}) collective-permute-start(f32[8,128]{1,0:T(8,128)S(1)} %get-tuple-element.26.own), channel_id=1, source_target_pairs={{1,2},{3,4},{5,6},{7,8},{9,10},{11,12},{13,14},{15,16},{17,18},{19... | collective-permute-start | bytes 12296 | tf_op jit(solution)/shard_map/ppermute | solution.py:551
  21.2 6.9 %collective-permute-start.4 = (f32[8,128]{1,0:T(8,128)S(1)}, f32[8,128]{1,0:T(8,128)S(1)}, u32[]{:S(2)}, u32[]{:S(2)}) collective-permute-start(f32[8,128]{1,0:T(8,128)S(1)} %get-tuple-element.26.own), channel_id=1, source_target_pairs={{0,1},{2,3},{4,5},{6,7},{8,9},{10,11},{12,13},{14,15},{16,17},{18,... | collective-permute-start | bytes 12296 | tf_op jit(solution)/shard_map/ppermute | solution.py:550

commit v7 on v6

--- a/solution.py
+++ b/solution.py
@@ -10,7 +10,7 @@
 RELAX = 0.8
 WET_MASS = 2e-05
 PAD = 8
-CHUNK = 16
+CHUNK = 8
 EAST, WEST, SOUTH, NORTH, MASS, RATE = range(6)
 
 
@@ -272,9 +272,9 @@
     set_rate(co2, 48)
     coarsen(co2, co3, 24, 4)
     set_rate(co3, 24)
-    first_sweep(t0, co0, b0, 0, 192)
-    sweep(t0, v0, co0, b0, 0, 192, 1)
-    residual(v0, r0, co0, b0, 0, 192, 1)
+    first_sweep(t0, co0, b0, 8, 184)
+    sweep(t0, v0, co0, b0, 8, 184, 1)
+    residual(v0, r0, co0, b0, 8, 184, 1)
     descend(
         v1, v2, b1, b2, b3, (co0, co1, co2), (r0, r1, r2), (t0, t1, t2), ((0, 192), (0, 96), (0, 48), (16, 32))
     )
@@ -414,15 +414,12 @@
     ascend(e3, (v0, v1, v2), (b0, b1, b2), (t0, t1, t2), (s0, s1, s2), co)
     second_descent(t0, b0, (v0a, v1a, v2a, b1a, b2a, bn), (r0, r1, r2), (s0, s1, s2), co)
     result = bn[0, 8:16, :]
-    place = lanes((8, 128))
-    slot = place & 7
+    slot = lanes((8, 128)) & 7
     out = jnp.where(slot == 0, result, jnp.where(slot == 1, responded[...], 0.0))
     mass = co3[MASS, 1, 16:24, :]
     sums = (mass, weight * b3[1, 16:24, :], weight * result, weight * responded[...])
     for k, value in enumerate(sums):
-        once = jnp.where(slot == 0, value, 0.0)
-        total = jnp.sum(jnp.sum(once, axis=0, keepdims=True), axis=1, keepdims=True)
-        out = jnp.where(place == 8 * k + 6, total, out)
+        out = jnp.where(slot == 2 + k, value, out)
     for z in range(packed.shape[0]):
         packed[z] = out
 
@@ -438,7 +435,11 @@
         total = total + gathered[k]
     slot = lanes((8, 128)) & 7
     value = jnp.where(slot < 2, own, jnp.where(slot < 4, pltpu.roll(before, 2, 1), pltpu.roll(after, 4, 1)))
-    value = jnp.where(slot < 6, value, total)
+    folded = total + pltpu.roll(total, 4, 0)
+    top = lax.broadcasted_iota(jnp.int32, (8, 128), 0) < 4
+    six = jnp.where(top, pltpu.roll(folded, 4, 1), pltpu.roll(folded, 3, 1))
+    seven = jnp.where(top, pltpu.roll(folded, 3, 1), pltpu.roll(folded, 2, 1))
+    value = jnp.where(slot < 6, value, jnp.where(slot == 6, six, seven))
     for k in range(out.shape[0]):
         out[k] = value
 
@@ -452,10 +453,14 @@
     total = gathered[0]
     for k in range(1, gathered.shape[0]):
         total = total + gathered[k]
-    place = lanes((1, 128))
-    mass, sum1, sum2a, sum2b = (
-        jnp.sum(jnp.where(place == 8 * k + 6, total[:1], 0.0), axis=1, keepdims=True) for k in range(4)
-    )
+    slot = lanes((8, 128)) & 7
+    top = lax.broadcasted_iota(jnp.int32, (8, 128), 0) < 4
+
+    def whole(k):
+        kept = jnp.where((slot == 6 + k // 2) & (top if k % 2 == 0 else ~top), total, 0.0)
+        return jnp.sum(jnp.sum(kept, axis=0, keepdims=True), axis=1, keepdims=True)
+
+    mass, sum1, sum2a, sum2b = (whole(k) for k in range(4))
     shift1 = RELAX * sum1 / mass
     shift2 = RELAX * (sum2a + shift1 * sum2b) / mass
 

time: 87.1 us -> 86.9 us (level)
  no operation moved by 1% of the time
where the time goes in v7:
time: 86.9 us; the launch traced here: 86.5 us
  blocking collectives  52.9 us (61%)
  starting transfers between devices  20.5 us (24%)
  Pallas kernels  9.65 us (11%)
  waiting for transfers between devices  2.68 us (3%)
    all_to_all x1, blocking collectives, shards(): gathered = lax.all_to_all(packed, 'z', 0, 0, tiled=True)  29.6 us
    all_to_all x1, blocking collectives, shards(): gathered = lax.all_to_all(gathered, ('grp', 'x'), 0, 0, tiled=True)  13.2 us
    all_to_all x1, blocking collectives, shards(): gathered = lax.all_to_all(gathered, 'grp', 0, 0, tiled=True)  10.1 us
    pallas_call x8, Pallas kernels, call(): pl.pallas_call(body, out_shape=outs, in_specs=[pl.BlockSpec(memory_space=...  9.65 us
    ppermute x1, starting transfers between devices, shards(): first = lax.ppermute(first, dev, swaps(0, 64))  6.4 us
    ppermute x1, starting transfers between devices, shards(): first = lax.ppermute(packed, dev, swaps(0, 64))  5.25 us
    ppermute x1, starting transfers between devices, shards(): far = lax.ppermute(far, 'grp', swaps(1, 8))  4.91 us
    ppermute x1, starting transfers between devices, shards(): near = lax.ppermute(near, 'grp', swaps(0, 8))  2.65 us
  transfers between devices with their start and end apart: 6, of which 3 were waited for; matrix products, arithmetic and copies ran while one was open for 0% of the time, Pallas kernels for 2%

profile of v7, /device:TPU:1, one launch (start us, length us, event | category | flops | bytes accessed | tf_op | source)
XLA Modules:
  0.0 86.5 jit_solution(10227850949343231968)
XLA Ops:
  0.6 1.0 %shard_map.68 = (f32[4,64,128]{2,1,0:T(8,128)S(1)}, f32[2,64,128]{2,1,0:T(8,128)S(1)}, f32[2,64,128]{2,1,0:T(8,128)S(1)}) custom-call(f32[64,128]{1,0:T(8,128)} %refs_0_.1, f32[64,128]{1,0:T(8,128)} %refs_1_.1, f32[64,128]{1,0:T(8,128)} %refs_2_.1, f32[64,128]{1,0:T(8,128)} %refs_3_.1, s32[64,128]{1,0:T(8,128)} %refs_4_.1), custom_call_target="tpu_custom_call" | custom-call | flops 2000000 | bytes 2000000 | tf_op jit(solution)/shard_map/pallas_call | solution.py:148
  1.6 0.7 collective-permute-start
  2.3 6.4 %collective-permute-start.1 = (f32[2,64,128]{2,1,0:T(8,128)S(1)}, f32[2,64,128]{2,1,0:T(8,128)S(1)}, u32[]{:S(2)}, u32[]{:S(2)}) collective-permute-start(f32[2,64,128]{2,1,0:T(8,128)S(1)} %get-tuple-element.22), channel_id=1, source_target_pairs={{0,1},{2,3},{4,5},{6,7},{8,9},{10,11},{12,13},{14,15},{16,17},{18,... | collective-permute-start | bytes 196616 | tf_op jit(solution)/shard_map/ppermute | solution.py:521
  8.7 0.0 collective-permute-done.second
  8.7 1.6 %collective-permute-done.1.first = f32[2,64,128]{2,1,0:T(8,128)S(1)} collective-permute-done((f32[2,64,128]{2,1,0:T(8,128)S(1)}, f32[2,64,128]{2,1,0:T(8,128)S(1)}, u32[]{:S(2)}, u32[]{:S(2)}) %collective-permute-start.1) | collective-permute-done | bytes 65568 | tf_op jit(solution)/shard_map/ppermute | solution.py:521
  10.3 0.2 shard_map.69
  10.5 4.9 %collective-permute-start.2 = (f32[2,176,128]{2,1,0:T(8,128)S(1)}, f32[2,176,128]{2,1,0:T(8,128)S(1)}, u32[]{:S(2)}, u32[]{:S(2)}) collective-permute-start(f32[2,176,128]{2,1,0:T(8,128)S(1)} %get-tuple-element.24), channel_id=1, source_target_pairs={{64,128},{192,256},{320,384},{128,64},{256,192},{384,320},{65,129}... | collective-permute-start | bytes 540680 | tf_op jit(solution)/shard_map/ppermute | solution.py:531
  15.5 2.7 %collective-permute-start.3 = (f32[2,176,128]{2,1,0:T(8,128)S(1)}, f32[2,176,128]{2,1,0:T(8,128)S(1)}, u32[]{:S(2)}, u32[]{:S(2)}) collective-permute-start(f32[2,176,128]{2,1,0:T(8,128)S(1)} %get-tuple-element.25), channel_id=1, source_target_pairs={{0,64},{128,192},{256,320},{384,448},{64,0},{192,128},{320,256},{4... | collective-permute-start | bytes 540680 | tf_op jit(solution)/shard_map/ppermute | solution.py:532
  18.1 0.5 collective-permute-done.2.far
  18.6 0.5 collective-permute-done.3.near
  19.2 1.4 %shard_map.70 = (f32[6,2,192,128]{3,2,1,0:T(8,128)S(1)}, f32[6,2,96,128]{3,2,1,0:T(8,128)S(1)}, f32[6,2,48,128]{3,2,1,0:T(8,128)S(1)}, f32[2,720,128]{2,1,0:T(8,...) custom-call(f32[2,256,128]{2,1,0:T(8,128)S(1)} %get-tuple-element.23.own, ...), custom_call_target="tpu_custom_call" | custom-call | flops 2000000 | bytes 2000000 | tf_op jit(solution)/shard_map/pallas_call | solution.py:148
  20.5 0.7 collective-permute-start.5
  21.2 5.2 %collective-permute-start.4 = (f32[8,128]{1,0:T(8,128)S(1)}, f32[8,128]{1,0:T(8,128)S(1)}, u32[]{:S(2)}, u32[]{:S(2)}) collective-permute-start(f32[8,128]{1,0:T(8,128)S(1)} %get-tuple-element.26.own), channel_id=1, source_target_pairs={{0,1},{2,3},{4,5},{6,7},{8,9},{10,11},{12,13},{14,15},{16,17},{18,... | collective-permute-start | bytes 12296 | tf_op jit(solution)/shard_map/ppermute | solution.py:555
  26.5 1.6 %shard_map.71 = (f32[2,720,128]{2,1,0:T(8,128)S(1)}, f32[8,128]{1,0:T(8,128)S(1)}) custom-call(f32[6,2,192,128]{3,2,1,0:T(8,128)S(1)} %get-tuple-element.27.co0, f32[6,2,96,128]{3,2,1,0:T(8,128)S(1)} %get-tuple-element.28.co1, f32[6,2,48,128]{3,2,1,0:T(8,128)S(1)} %get-tuple-element.29.co2, f32[6,2,24,128]{3,2,1,0:T(8,128)S(1)} %get-tuple-element.30.co3), custom_call_target="tpu_custom_call" | custom-call | flops 6000000 | bytes 6000000 | tf_op jit(solution)/shard_map/pallas_call | solution.py:148
  28.1 0.0 collective-permute-done.5.second
  28.1 0.0 collective-permute-done.4.first
  28.1 0.1 shard_map.72
  28.2 10.1 %all_to_all.15.gathered = f32[8,2,8,128]{3,2,1,0:T(8,128)S(1)} all-to-all(f32[8,2,8,128]{3,2,1,0:T(8,128)S(1)} %shard_map.72), channel_id=1, replica_groups=mesh['grp'=8,'z'=16,'x'=4] {'grp'}, dimensions={0} | all-to-all | bytes 131072 | tf_op jit(solution)/shard_map/all_to_all | solution.py:566
  38.3 3.0 %shard_map.73 = (f32[6,3,40,128]{3,2,1,0:T(8,128)S(1)}, f32[6,3,24,128]{3,2,1,0:T(8,128)S(1)}, f32[2,720,128]{2,1,0:T(8,128)S(1)}, f32[16,8,128]{2,1,0:T(8,128)S(1)}) custom-call(f32[8,2,8,128]{3,2,1,0:T(8,128)S(1)} %all_to_all.15.gathered, f32[8,128]{1,0:T(8,128)S(1)} %get-tuple-element.31.responded, f32[6,2,192,128]{3,2,1,0:T(8,128)S(1)} %get-tuple-element.27.co0, ...), custom_call_target="tpu_custom_call" | custom-call | flops 2000000 | bytes 2000000 | tf_op jit(solution)/shard_map/pallas_call | solution.py:148
  41.2 29.6 %all_to_all.16.gathered = f32[16,8,128]{2,1,0:T(8,128)S(1)} all-to-all(f32[16,8,128]{2,1,0:T(8,128)S(1)} %get-tuple-element.33), channel_id=1, replica_groups=mesh['grp'=8,'z'=16,'x'=4] {'z'}, dimensions={0} | all-to-all | bytes 131072 | tf_op jit(solution)/shard_map/all_to_all | solution.py:586
  70.8 0.1 shard_map.74
  70.9 13.2 %all_to_all.17.gathered = f32[32,8,128]{2,1,0:T(8,128)S(1)} all-to-all(f32[32,8,128]{2,1,0:T(8,128)S(1)} %shard_map.74), channel_id=1, replica_groups=mesh['grp'=8,'z'=16,'x'=4] {'grp','x'}, dimensions={0} | all-to-all | bytes 262144 | tf_op jit(solution)/shard_map/all_to_all | solution.py:588
  84.1 2.3 %shard_map.75 = (f32[64,128]{1,0:T(8,128)}, f32[64,128]{1,0:T(8,128)}) custom-call(f32[32,8,128]{2,1,0:T(8,128)S(1)} %all_to_all.17.gathered, f32[2,256,128]{2,1,0:T(8,128)S(1)} %get-tuple-element.23.own, f32[6,2,192,128]{3,2,1,0:T(8,128)S(1)} %get-tuple-element.27.co0, f32[6,2,96,128]{3,2,1,0:T(8,128)S(1)} %get-tuple-element.28.co1, ...), custom_call_target="tpu_custom_call" | custom-call | flops 2000000 | bytes 2000000 | tf_op jit(solution)/shard_map/pallas_call | solution.py:148
Async XLA Ops:
  1.6 7.1 %collective-permute-start = (f32[2,64,128]{2,1,0:T(8,128)S(1)}, f32[2,64,128]{2,1,0:T(8,128)S(1)}, u32[]{:S(2)}, u32[]{:S(2)}) collective-permute-start(f32[2,64,128]{2,1,0:T(8,128)S(1)} %get-tuple-element.21), channel_id=1, source_target_pairs={{1,2},{3,4},{5,6},{7,8},{9,10},{11,12},{13,14},{15,16},{17,18},{19... | collective-permute-start | bytes 196616 | tf_op jit(solution)/shard_map/ppermute | solution.py:522
  2.3 8.1 %collective-permute-start.1 = (f32[2,64,128]{2,1,0:T(8,128)S(1)}, f32[2,64,128]{2,1,0:T(8,128)S(1)}, u32[]{:S(2)}, u32[]{:S(2)}) collective-permute-start(f32[2,64,128]{2,1,0:T(8,128)S(1)} %get-tuple-element.22), channel_id=1, source_target_pairs={{0,1},{2,3},{4,5},{6,7},{8,9},{10,11},{12,13},{14,15},{16,17},{18,... | collective-permute-start | bytes 196616 | tf_op jit(solution)/shard_map/ppermute | solution.py:521
  10.5 8.1 %collective-permute-start.2 = (f32[2,176,128]{2,1,0:T(8,128)S(1)}, f32[2,176,128]{2,1,0:T(8,128)S(1)}, u32[]{:S(2)}, u32[]{:S(2)}) collective-permute-start(f32[2,176,128]{2,1,0:T(8,128)S(1)} %get-tuple-element.24), channel_id=1, source_target_pairs={{64,128},{192,256},{320,384},{128,64},{256,192},{384,320},{65,129}... | collective-permute-start | bytes 540680 | tf_op jit(solution)/shard_map/ppermute | solution.py:531
  15.5 3.7 %collective-permute-start.3 = (f32[2,176,128]{2,1,0:T(8,128)S(1)}, f32[2,176,128]{2,1,0:T(8,128)S(1)}, u32[]{:S(2)}, u32[]{:S(2)}) collective-permute-start(f32[2,176,128]{2,1,0:T(8,128)S(1)} %get-tuple-element.25), channel_id=1, source_target_pairs={{0,64},{128,192},{256,320},{384,448},{64,0},{192,128},{320,256},{4... | collective-permute-start | bytes 540680 | tf_op jit(solution)/shard_map/ppermute | solution.py:532
  20.5 7.5 %collective-permute-start.5 = (f32[8,128]{1,0:T(8,128)S(1)}, f32[8,128]{1,0:T(8,128)S(1)}, u32[]{:S(2)}, u32[]{:S(2)}) collective-permute-start(f32[8,128]{1,0:T(8,128)S(1)} %get-tuple-element.26.own), channel_id=1, source_target_pairs={{1,2},{3,4},{5,6},{7,8},{9,10},{11,12},{13,14},{15,16},{17,18},{19... | collective-permute-start | bytes 12296 | tf_op jit(solution)/shard_map/ppermute | solution.py:556
  21.2 6.9 %collective-permute-start.4 = (f32[8,128]{1,0:T(8,128)S(1)}, f32[8,128]{1,0:T(8,128)S(1)}, u32[]{:S(2)}, u32[]{:S(2)}) collective-permute-start(f32[8,128]{1,0:T(8,128)S(1)} %get-tuple-element.26.own), channel_id=1, source_target_pairs={{0,1},{2,3},{4,5},{6,7},{8,9},{10,11},{12,13},{14,15},{16,17},{18,... | collective-permute-start | bytes 12296 | tf_op jit(solution)/shard_map/ppermute | solution.py:555
